TPU v7x, 128 devices: a whole 4x4x4 slice. The times are simulated.
128 devices in a mesh: pipe: 2 (over x_hi), ctx: 8 (over x_lo, z), tp: 8 (over y, core).
Axes of the slice: x: 4 (x_hi: 2, x_lo: 2; x = x_hi * 2 + x_lo), y: 4, z: 4, core: 2. Of those that a mesh axis runs over, the one named last changes fastest.
Arguments:
- queries: bfloat16 [2, 2, 4096, 8192], P('pipe', None, 'ctx', 'tp'), may hold values from -220 to 220
- keys: bfloat16 [2, 2, 4096, 1024], P('pipe', None, 'ctx', 'tp'), may hold values from -8 to 8
- values: bfloat16 [2, 2, 4096, 1024], P('pipe', None, 'ctx', 'tp'), may hold values from -16 to 16
- doc_start: int32 [2, 4096], P(None, 'ctx'), may hold values from 0 to 4095, as said below
- owners: int32 [2, 128], P(None, 'ctx'), may hold values from 0 to 7, as said below
Outputs:
- balanced: bfloat16 [2, 2, 8, 8, 3, 32, 8192], P('pipe', None, 'ctx', None, None, None, 'tp')
Inputs may be any that keep to these rules, and one draw needn't show every extreme that they name: doc_start[m, i] is the first token of token i's document: it never decreases along the slab, is at most i, i - doc_start[m, i] < 256, and every slab holds a document of exactly 256 tokens. `owners`: of the 16 tracts that lie on one index of ctx, at most 3 have the same owner, and in every such block some owner gets exactly 3.
All inputs are finite; a program needn't handle non-finite values.
Results may differ from a plain program's by a relative error of at most 0.0063.
Values may be sent and summed in bfloat16 or wider, within the bound.
A program may use at most 128 MiB of HBM per device.

v0:
```python
import math

import jax
import jax.numpy as jnp
from jax import lax
from jax.sharding import PartitionSpec as P

HEAD_WIDTH = 128
TRACTS_DEV = 16
DOCMAX = 256


def shifted(block, axis, distance):
    devices = range(lax.axis_size(axis))
    route = [(i - distance, i) for i in devices if i - distance in devices]
    return lax.ppermute(block, axis, route)


def rank_table(owner_list, owner_count, slot_count):
    tract_count = owner_list.shape[0]
    positions = jnp.arange(tract_count, dtype=jnp.int32)
    earlier = positions[None, :] < positions[:, None]
    same_owner = owner_list[:, None] == owner_list[None, :]
    rank_of = jnp.sum(same_owner & earlier, axis=1)
    owner_ids = jnp.arange(owner_count, dtype=jnp.int32)
    slot_ids = jnp.arange(slot_count, dtype=jnp.int32)
    return (owner_list[None, None, :] == owner_ids[:, None, None]) & (
        rank_of[None, None, :] == slot_ids[None, :, None]
    )


def attend_rows(query_rows, key_win, value_win, first_key, row_ids, row_starts):
    query_count = query_rows.shape[0]
    key_span = key_win.shape[0]
    kv_heads = key_win.shape[1] // HEAD_WIDTH
    query_group_width = query_rows.shape[1] // (kv_heads * HEAD_WIDTH)
    heads_for_query = query_rows.reshape(query_count, kv_heads, query_group_width, HEAD_WIDTH)
    heads_for_key = key_win.reshape(key_span, kv_heads, HEAD_WIDTH)
    value_heads = value_win.reshape(key_span, kv_heads, HEAD_WIDTH)
    scores = jnp.einsum(
        "tkgd,jkd->tkgj", heads_for_query, heads_for_key, preferred_element_type=jnp.float32
    ) / math.sqrt(HEAD_WIDTH)
    key_ids = first_key + jnp.arange(key_span, dtype=jnp.int32)
    allowed = (key_ids[None, :] >= row_starts[:, None]) & (key_ids[None, :] <= row_ids[:, None])
    scores = jnp.where(allowed[:, None, None, :], scores, -1e30)
    row_max = jnp.max(scores, axis=-1, keepdims=True)
    exp_terms = jnp.exp(scores - row_max)
    denom_sum = jnp.sum(exp_terms, axis=-1)
    weights = exp_terms.astype(jnp.bfloat16)
    attended = (
        jnp.einsum("tkgj,jkd->tkgd", weights, value_heads, preferred_element_type=jnp.float32)
        / denom_sum[..., None]
    )
    return attended.reshape(query_count, -1).astype(jnp.bfloat16)


def local(queries, keys, values, doc_start, owners):
    section_index = lax.axis_index("pipe")
    my_ctx = lax.axis_index("ctx")
    ctx_count = lax.axis_size("ctx")
    micro_count = queries.shape[1]
    rows_dev = queries.shape[2]
    width_q = queries.shape[3]
    width_kv = keys.shape[3]
    tract_rows = rows_dev // TRACTS_DEV
    slot_count = TRACTS_DEV // ctx_count + 1
    local_ids = jnp.arange(tract_rows, dtype=jnp.int32)
    carried = jnp.zeros((ctx_count, slot_count, tract_rows, width_q), jnp.bfloat16)
    tick_outputs = []
    for clock_tick in range(micro_count + 1):
        mb_index = clock_tick - section_index
        mb_pick = jnp.clip(mb_index, 0, micro_count - 1)
        own_queries = lax.dynamic_index_in_dim(queries[0], mb_pick, 0, keepdims=False)
        key_rows = lax.dynamic_index_in_dim(keys[0], mb_pick, 0, keepdims=False)
        value_rows = lax.dynamic_index_in_dim(values[0], mb_pick, 0, keepdims=False)
        own_list = lax.dynamic_index_in_dim(owners, mb_pick, 0, keepdims=False)
        send_map = rank_table(own_list, ctx_count, slot_count).astype(jnp.bfloat16)
        tract_block = own_queries.reshape(TRACTS_DEV, tract_rows, width_q)
        outgoing = jnp.einsum(
            "osk,ktf->ostf", send_map, tract_block, preferred_element_type=jnp.float32
        ).astype(jnp.bfloat16)
        arrived = lax.all_to_all(outgoing, "ctx", split_axis=0, concat_axis=0, tiled=True)
        all_keys, all_values, all_owners, all_starts = (
            lax.all_gather(key_rows, "ctx", axis=0, tiled=True),
            lax.all_gather(value_rows, "ctx", axis=0, tiled=True),
            lax.all_gather(owners, "ctx", axis=1, tiled=True),
            lax.all_gather(doc_start, "ctx", axis=1, tiled=True),
        )
        section_in = (arrived.astype(jnp.float32) + carried.astype(jnp.float32)).astype(
            jnp.bfloat16
        )
        lists = lax.dynamic_index_in_dim(all_owners, mb_pick, 0, keepdims=False).reshape(
            ctx_count, TRACTS_DEV
        )
        starts_all = lax.dynamic_index_in_dim(all_starts, mb_pick, 0, keepdims=False)

        def table_of(block_list):
            return rank_table(block_list, ctx_count, slot_count)

        tables = jax.vmap(table_of)(lists)
        mine = lax.dynamic_index_in_dim(tables, my_ctx, 1, keepdims=False)
        present = jnp.any(mine, axis=2)
        tract_pos = jnp.sum(
            mine.astype(jnp.int32) * jnp.arange(TRACTS_DEV, dtype=jnp.int32), axis=2
        )
        first_rows = (
            jnp.arange(ctx_count, dtype=jnp.int32)[:, None] * rows_dev + tract_pos * tract_rows
        )
        row_grid = first_rows[..., None] + local_ids
        start_grid = starts_all[row_grid]
        padded_keys = jnp.concatenate(
            [jnp.zeros((DOCMAX, width_kv), jnp.bfloat16), all_keys], axis=0
        )
        padded_values = jnp.concatenate(
            [jnp.zeros((DOCMAX, width_kv), jnp.bfloat16), all_values], axis=0
        )
        source_answers = []
        for source_id in range(ctx_count):
            key_win = padded_keys[source_id * rows_dev : source_id * rows_dev + rows_dev + DOCMAX]
            value_win = padded_values[
                source_id * rows_dev : source_id * rows_dev + rows_dev + DOCMAX
            ]
            slot_queries = section_in[source_id].reshape(slot_count * tract_rows, width_q)
            slot_ids = row_grid[source_id].reshape(-1)
            slot_starts = start_grid[source_id].reshape(-1)
            answer = attend_rows(
                slot_queries,
                key_win,
                value_win,
                source_id * rows_dev - DOCMAX,
                slot_ids,
                slot_starts,
            )
            source_answers.append(answer.reshape(slot_count, tract_rows, width_q))
        answers = jnp.stack(source_answers)
        owner_rows = jnp.where(present[:, :, None, None], answers, jnp.zeros_like(answers))
        if clock_tick < micro_count:
            carried = shifted(owner_rows, "pipe", 1)
        tick_outputs.append(owner_rows)
    first_section = section_index == 0
    result = jnp.stack(
        [
            jnp.where(first_section, tick_outputs[micro_id], tick_outputs[micro_id + 1])
            for micro_id in range(micro_count)
        ]
    )
    return result[None, :, None]


def solution(mesh):
    return jax.shard_map(
        local,
        mesh=mesh,
        in_specs=(
            P("pipe", None, "ctx", "tp"),
            P("pipe", None, "ctx", "tp"),
            P("pipe", None, "ctx", "tp"),
            P(None, "ctx"),
            P(None, "ctx"),
        ),
        out_specs=P("pipe", None, "ctx", None, None, None, "tp"),
        check_vma=False,
    )
```

profile of v0, /device:TPU:20, one launch (start us, length us, event | category | flops | bytes accessed | tf_op | source)
XLA Modules:
  0.0 336.1 jit_solution(15088686143844010737)
XLA Ops:
  6.5 1.9 constant_dynamic-slice_fusion.16
  8.6 1.8 constant_dynamic-slice_fusion.4
  12.7 1.7 constant_dynamic-slice_fusion
  15.3 2.0 copy.204
  17.3 6.1 %all-to-all-start = ((bf16[8,3,32,1024]{3,2,1,0:T(8,128)(2,1)}), bf16[8,3,32,1024]{3,2,1,0:T(8,128)(2,1)S(1)}, u32[]{:S(2)}, u32[]{:S(2)}) async-start(bf16[8,3,32,1024]{3,2,1,0:T(8,128)(2,1)} %copy.204), calls=%async_computation | async-start | bytes 3145728 | tf_op jit(solution)/shard_map/all_to_all | solution.py:82
  24.0 36.9 %all-gather.6 = s32[8,16,2]{1,2,0:T(2,128)S(1)} all-gather(s32[1,16,2]{1,2,0:T(2,128)S(1)} %bitcast.1570), channel_id=1, replica_groups=mesh['pipe'=2,'ctx'=8,'tp'=8] {'ctx'}, dimensions={0}, use_global_device_ids=true | all-gather | bytes 1152 | tf_op jit(solution)/shard_map/all_gather | solution.py:86
  63.5 28.1 %all_gather.30 = s32[2,4096]{1,0:T(2,128)S(1)} all-gather(s32[2,512]{1,0:T(2,128)S(1)} %copy-done.96), channel_id=1, replica_groups=mesh['pipe'=2,'ctx'=8,'tp'=8] {'ctx'}, dimensions={1}, use_global_device_ids=true | all-gather | bytes 36864 | tf_op jit(solution)/shard_map/all_gather | solution.py:87
  91.6 4.5 %gather_fusion.1 = s32[768]{0:T(1024)S(1)} fusion(s32[4096]{0:T(1024)S(1)} %bitcast.1515, s32[1024]{0:T(1024)S(1)} %pad_clamp_fusion.1), kind=kCustom, calls=%fused_computation.1 | custom fusion | bytes 9216 | tf_op jit(solution)/shard_map/gather | solution.py:110
  96.3 4.5 %gather_fusion = s32[768]{0:T(1024)S(1)} fusion(s32[4096]{0:T(1024)S(1)} %bitcast.1514, s32[1024]{0:T(1024)S(1)} %pad_clamp_fusion.2), kind=kCustom, calls=%fused_computation | custom fusion | bytes 9216 | tf_op jit(solution)/shard_map/gather | solution.py:110
  101.2 4.9 %gather_fusion.2 = s32[768]{0:T(1024)S(1)} fusion(s32[4096]{0:T(1024)S(1)} %bitcast.1513, s32[1024]{0:T(1024)S(1)} %pad_clamp_fusion), kind=kCustom, calls=%fused_computation.2 | custom fusion | bytes 9216 | tf_op jit(solution)/shard_map/gather | solution.py:110
  122.8 1.5 fusion.48
  124.3 1.3 fusion
  125.6 1.8 fusion.429
  127.6 1.6 fusion.49
  142.7 1.4 fusion.408
  149.2 1.0 constant_dynamic-update-slice_fusion.11
  152.1 1.3 broadcast_select_fusion.1
  153.5 1.3 collective-permute-start
  155.7 2.0 copy.225
  157.7 3.7 %all-to-all-start.1 = ((bf16[8,3,32,1024]{3,2,1,0:T(8,128)(2,1)}), bf16[8,3,32,1024]{3,2,1,0:T(8,128)(2,1)S(1)}, u32[]{:S(2)}, u32[]{:S(2)}) async-start(bf16[8,3,32,1024]{3,2,1,0:T(8,128)(2,1)} %copy.225), calls=%async_computation.1 | async-start | bytes 3145728 | tf_op jit(solution)/shard_map/all_to_all | solution.py:82
  163.8 2.0 copy.255
  169.0 11.0 %all-to-all-done.1 = bf16[8,3,32,1024]{3,2,1,0:T(8,128)(2,1)S(1)} async-done(((bf16[8,3,32,1024]{3,2,1,0:T(8,128)(2,1)}), bf16[8,3,32,1024]{3,2,1,0:T(8,128)(2,1)S(1)}, u32[]{:S(2)}, u32[]{:S(2)}) %all-to-all-start.1) | async-done | bytes 1572896 | tf_op jit(solution)/shard_map/all_to_all | solution.py:82
  180.0 4.7 %all-to-all-start.2 = ((bf16[8,3,32,1024]{3,2,1,0:T(8,128)(2,1)}), bf16[8,3,32,1024]{3,2,1,0:T(8,128)(2,1)}, u32[]{:S(2)}, u32[]{:S(2)}) async-start(bf16[8,3,32,1024]{3,2,1,0:T(8,128)(2,1)} %copy.255), calls=%async_computation.2 | async-start | bytes 3145728 | tf_op jit(solution)/shard_map/all_to_all | solution.py:82
  184.7 15.8 %collective-permute-done = bf16[8,3,32,1024]{3,2,1,0:T(8,128)(2,1)} collective-permute-done((bf16[8,3,32,1024]{3,2,1,0:T(8,128)(2,1)}, bf16[8,3,32,1024]{3,2,1,0:T(8,128)(2,1)}, u32[]{:S(2)}, u32[]{:S(2)}) %collective-permute-start) | collective-permute-done | bytes 1572896 | tf_op jit(solution)/shard_map/ppermute | solution.py:16
  200.5 2.1 add_convert_fusion.1
  202.6 1.1 fusion.571
  203.8 1.6 fusion.57
  206.0 1.3 fusion.18
  207.2 1.7 fusion.402
  214.5 1.7 fusion.399
  217.8 1.7 fusion.396
  221.8 1.7 fusion.393
  225.9 1.7 fusion.390
  229.9 1.7 fusion.387
  233.8 1.7 fusion.384
  236.7 1.3 broadcast_select_fusion
  238.0 1.4 collective-permute-start.1
  250.5 44.4 %collective-permute-done.1 = bf16[8,3,32,1024]{3,2,1,0:T(8,128)(2,1)} collective-permute-done((bf16[8,3,32,1024]{3,2,1,0:T(8,128)(2,1)}, bf16[8,3,32,1024]{3,2,1,0:T(8,128)(2,1)}, u32[]{:S(2)}, u32[]{:S(2)}) %collective-permute-start.1) | collective-permute-done | bytes 1572896 | tf_op jit(solution)/shard_map/ppermute | solution.py:16
  294.9 2.6 add_convert_fusion
  297.5 1.1 fusion.570
  298.7 1.6 fusion.71
  300.8 1.3 fusion.46
  302.1 1.7 fusion.360
  313.5 1.7 fusion.372
  316.8 1.7 fusion.375
  320.1 1.7 fusion.378
  324.8 2.3 select_select_fusion.1
  327.1 1.9 maximum_bitcast_fusion
  (507 shorter events, 94.4 us)
Async XLA Ops:
  6.5 6.1 %copy-start.3 = (bf16[1,2,512,1024]{3,2,1,0:T(8,128)(2,1)S(1)}, bf16[1,2,512,1024]{3,2,1,0:T(8,128)(2,1)}, u32[]{:S(2)}) copy-start(bf16[1,2,512,1024]{3,2,1,0:T(8,128)(2,1)} %param.5) | copy-start | bytes 6291460
  6.5 116.3 %all-gather.16.cloned.1.call-start = ((), (), s32[]{:S(2)}) async-start(), calls=%async_computation.4 | async-start | bytes 1179648 | tf_op jit(solution)/shard_map/all_gather | solution.py:84
  8.5 117.1 %all-gather.14.cloned.1.call-start = ((), (), s32[]{:S(2)}) async-start(), calls=%async_computation.3 | async-start | bytes 1179648 | tf_op jit(solution)/shard_map/all_gather | solution.py:85
  10.4 193.4 %all-gather.20.cloned.1.call-start = ((), (), s32[]{:S(2)}) async-start(), calls=%async_computation.6 | async-start | bytes 1179648 | tf_op jit(solution)/shard_map/all_gather | solution.py:84
  11.1 196.1 %all-gather.18.cloned.1.call-start = ((), (), s32[]{:S(2)}) async-start(), calls=%async_computation.5 | async-start | bytes 1179648 | tf_op jit(solution)/shard_map/all_gather | solution.py:85
  17.3 6.7 %copy-start.89 = (s32[2,16]{1,0:T(2,128)S(1)}, s32[2,16]{1,0:T(2,128)}, u32[]{:S(2)}) copy-start(s32[2,16]{1,0:T(2,128)} %param.9) | copy-start | bytes 388
  17.3 46.2 %copy-start.96 = (s32[2,512]{1,0:T(2,128)S(1)}, s32[2,512]{1,0:T(2,128)}, u32[]{:S(2)}) copy-start(s32[2,512]{1,0:T(2,128)} %param.8) | copy-start | bytes 12292
  17.3 100.4 %all-to-all-start = ((bf16[8,3,32,1024]{3,2,1,0:T(8,128)(2,1)}), bf16[8,3,32,1024]{3,2,1,0:T(8,128)(2,1)S(1)}, u32[]{:S(2)}, u32[]{:S(2)}) async-start(bf16[8,3,32,1024]{3,2,1,0:T(8,128)(2,1)} %copy.204), calls=%async_computation | async-start | bytes 3145728 | tf_op jit(solution)/shard_map/all_to_all | solution.py:82
  23.4 275.3 %all-gather.24.cloned.1.call-start = ((), (), s32[]{:S(2)}) async-start(), calls=%async_computation.8 | async-start | bytes 1179648 | tf_op jit(solution)/shard_map/all_gather | solution.py:84
  117.8 5.0 %copy-start.77 = (pred[96,768]{1,0:T(8,128)(4,1)S(1)}, pred[96,768]{1,0:T(8,128)(4,1)}, u32[]{:S(2)}) copy-start(pred[96,768]{1,0:T(8,128)(4,1)} %get-tuple-element.103) | copy-start | bytes 221188
  144.6 5.6 %copy-start.6 = (bf16[96,1,8,128]{3,2,0,1:T(8,128)(2,1)}, bf16[96,1,8,128]{3,2,0,1:T(8,128)(2,1)S(1)}, u32[]{:S(2)}) copy-start(bf16[96,1,8,128]{3,2,0,1:T(8,128)(2,1)S(1)} %copy.212) | copy-start | bytes 589828
  144.8 7.3 %copy-start.8 = (bf16[96,1,8,128]{3,2,0,1:T(8,128)(2,1)}, bf16[96,1,8,128]{3,2,0,1:T(8,128)(2,1)S(1)}, u32[]{:S(2)}) copy-start(bf16[96,1,8,128]{3,2,0,1:T(8,128)(2,1)S(1)} %copy.214) | copy-start | bytes 589828
  145.6 7.8 %copy-start.10 = (bf16[96,1,8,128]{3,2,0,1:T(8,128)(2,1)}, bf16[96,1,8,128]{3,2,0,1:T(8,128)(2,1)S(1)}, u32[]{:S(2)}) copy-start(bf16[96,1,8,128]{3,2,0,1:T(8,128)(2,1)S(1)} %copy.216) | copy-start | bytes 589828
  145.6 6.5 %copy-start.90 = (pred[8,3]{1,0:T(8,128)(4,1)S(1)}, pred[8,3]{1,0:T(8,128)(4,1)}, u32[]{:S(2)}) copy-start(pred[8,3]{1,0:T(8,128)(4,1)} %copy.200) | copy-start | bytes 76
  146.5 7.0 %copy-start.12 = (bf16[96,1,8,128]{3,2,0,1:T(8,128)(2,1)}, bf16[96,1,8,128]{3,2,0,1:T(8,128)(2,1)S(1)}, u32[]{:S(2)}) copy-start(bf16[96,1,8,128]{3,2,0,1:T(8,128)(2,1)S(1)} %copy.218) | copy-start | bytes 589828
  148.3 5.2 %copy-start.14 = (bf16[96,1,8,128]{3,2,0,1:T(8,128)(2,1)}, bf16[96,1,8,128]{3,2,0,1:T(8,128)(2,1)S(1)}, u32[]{:S(2)}) copy-start(bf16[96,1,8,128]{3,2,0,1:T(8,128)(2,1)S(1)} %copy.220) | copy-start | bytes 589828
  149.1 3.0 copy-start.49
  149.1 5.6 %copy-start.5 = (bf16[1,1,512,1024]{3,2,1,0:T(8,128)(2,1)S(1)}, bf16[1,1,512,1024]{3,2,1,0:T(8,128)(2,1)}, u32[]{:S(2)}) copy-start(bf16[1,1,512,1024]{3,2,1,0:T(8,128)(2,1)} %get-tuple-element.13) | copy-start | bytes 3145732
  149.1 5.6 %copy-start.95 = (pred[8,16]{1,0:T(8,128)(4,1)S(1)}, pred[8,16]{1,0:T(8,128)(4,1)}, u32[]{:S(2)}) copy-start(pred[8,16]{1,0:T(8,128)(4,1)} %get-tuple-element.182) | copy-start | bytes 388
  149.2 5.6 %copy-start.99 = (pred[3,16]{1,0:T(4,128)(4,1)S(1)}, pred[3,16]{1,0:T(4,128)(4,1)}, u32[]{:S(2)}) copy-start(pred[3,16]{1,0:T(4,128)(4,1)} %iota_compare_fusion.11) | copy-start | bytes 148
  153.5 47.0 %collective-permute-start = (bf16[8,3,32,1024]{3,2,1,0:T(8,128)(2,1)}, bf16[8,3,32,1024]{3,2,1,0:T(8,128)(2,1)}, u32[]{:S(2)}, u32[]{:S(2)}) collective-permute-start(bf16[8,3,32,1024]{3,2,1,0:T(8,128)(2,1)} %broadcast_select_fusion.1), channel_id=1, source_target_pairs={{0,64},{1,65},{2,66},{3,67},{4,68},{5,69},{6,70},{7,71},{8,72},{9,... | collective-permute-start | bytes 4718600 | tf_op jit(solution)/shard_map/ppermute | solution.py:16
  157.7 4.3 %copy-start.81 = (pred[8,3,16]{2,0,1:T(8,128)(4,1)S(1)}, pred[8,3,16]{2,0,1:T(8,128)(4,1)}, u32[]{:S(2)}) copy-start(pred[8,3,16]{2,0,1:T(8,128)(4,1)} %copy-done.80) | copy-start | bytes 1156
  157.7 4.3 %copy-start.88 = (pred[8,1,16]{2,0,1:T(8,128)(4,1)S(1)}, pred[8,1,16]{2,0,1:T(8,128)(4,1)}, u32[]{:S(2)}) copy-start(pred[8,1,16]{2,0,1:T(8,128)(4,1)} %copy-done.87) | copy-start | bytes 388
  157.7 5.1 %copy-start.98 = (s32[16]{0:T(128)S(1)}, s32[16]{0:T(128)}, u32[]{:S(2)}) copy-start(s32[16]{0:T(128)} %get-tuple-element.179) | copy-start | bytes 196
  157.7 5.1 %copy-start.4 = (bf16[1,1,512,1024]{3,2,1,0:T(8,128)(2,1)S(1)}, bf16[1,1,512,1024]{3,2,1,0:T(8,128)(2,1)}, u32[]{:S(2)}) copy-start(bf16[1,1,512,1024]{3,2,1,0:T(8,128)(2,1)} %get-tuple-element.11) | copy-start | bytes 3145732
  157.7 5.1 %copy-start.94 = (pred[8,16]{1,0:T(8,128)(4,1)S(1)}, pred[8,16]{1,0:T(8,128)(4,1)}, u32[]{:S(2)}) copy-start(pred[8,16]{1,0:T(8,128)(4,1)} %get-tuple-element.181) | copy-start | bytes 388
  157.7 22.3 %all-to-all-start.1 = ((bf16[8,3,32,1024]{3,2,1,0:T(8,128)(2,1)}), bf16[8,3,32,1024]{3,2,1,0:T(8,128)(2,1)S(1)}, u32[]{:S(2)}, u32[]{:S(2)}) async-start(bf16[8,3,32,1024]{3,2,1,0:T(8,128)(2,1)} %copy.225), calls=%async_computation.1 | async-start | bytes 3145728 | tf_op jit(solution)/shard_map/all_to_all | solution.py:82
  161.4 140.7 %all-gather.22.cloned.1.call-start = ((), (), s32[]{:S(2)}) async-start(), calls=%async_computation.7 | async-start | bytes 1179648 | tf_op jit(solution)/shard_map/all_gather | solution.py:85
  162.8 2.9 copy-start.79
  162.9 2.9 copy-start.86
  163.7 3.7 %copy-start.19 = (bf16[96,1,8,128]{3,2,0,1:T(8,128)(2,1)S(1)}, bf16[96,1,8,128]{3,2,0,1:T(8,128)(2,1)}, u32[]{:S(2)}) copy-start(bf16[96,1,8,128]{3,2,0,1:T(8,128)(2,1)} %copy-done.18) | copy-start | bytes 589828
  180.0 70.5 %all-to-all-start.2 = ((bf16[8,3,32,1024]{3,2,1,0:T(8,128)(2,1)}), bf16[8,3,32,1024]{3,2,1,0:T(8,128)(2,1)}, u32[]{:S(2)}, u32[]{:S(2)}) async-start(bf16[8,3,32,1024]{3,2,1,0:T(8,128)(2,1)} %copy.255), calls=%async_computation.2 | async-start | bytes 3145728 | tf_op jit(solution)/shard_map/all_to_all | solution.py:82
  207.2 2.9 copy-start.76
  235.9 3.6 %copy-start.44 = (bf16[1,1,3,32,1024]{4,3,2,1,0:T(8,128)(2,1)S(1)}, bf16[1,1,3,32,1024]{4,3,2,1,0:T(8,128)(2,1)}, u32[]{:S(2)}) copy-start(bf16[1,1,3,32,1024]{4,3,2,1,0:T(8,128)(2,1)} %stack.68) | copy-start | bytes 589828
  236.5 3.7 %copy-start.15 = (bf16[96,1,8,128]{3,2,0,1:T(8,128)(2,1)S(1)}, bf16[96,1,8,128]{3,2,0,1:T(8,128)(2,1)}, u32[]{:S(2)}) copy-start(bf16[96,1,8,128]{3,2,0,1:T(8,128)(2,1)} %copy-done.14) | copy-start | bytes 589828
  236.6 3.7 %copy-start.13 = (bf16[96,1,8,128]{3,2,0,1:T(8,128)(2,1)S(1)}, bf16[96,1,8,128]{3,2,0,1:T(8,128)(2,1)}, u32[]{:S(2)}) copy-start(bf16[96,1,8,128]{3,2,0,1:T(8,128)(2,1)} %copy-done.12) | copy-start | bytes 589828
  236.6 3.8 %copy-start.11 = (bf16[96,1,8,128]{3,2,0,1:T(8,128)(2,1)S(1)}, bf16[96,1,8,128]{3,2,0,1:T(8,128)(2,1)}, u32[]{:S(2)}) copy-start(bf16[96,1,8,128]{3,2,0,1:T(8,128)(2,1)} %copy-done.10) | copy-start | bytes 589828
  236.6 3.8 %copy-start.9 = (bf16[96,1,8,128]{3,2,0,1:T(8,128)(2,1)S(1)}, bf16[96,1,8,128]{3,2,0,1:T(8,128)(2,1)}, u32[]{:S(2)}) copy-start(bf16[96,1,8,128]{3,2,0,1:T(8,128)(2,1)} %copy-done.8) | copy-start | bytes 589828
  236.7 3.9 %copy-start.7 = (bf16[96,1,8,128]{3,2,0,1:T(8,128)(2,1)S(1)}, bf16[96,1,8,128]{3,2,0,1:T(8,128)(2,1)}, u32[]{:S(2)}) copy-start(bf16[96,1,8,128]{3,2,0,1:T(8,128)(2,1)} %copy-done.6) | copy-start | bytes 589828
  238.0 6.2 %copy-start.31 = (bf16[96,1,8,128]{3,2,0,1:T(8,128)(2,1)S(1)}, bf16[96,1,8,128]{3,2,0,1:T(8,128)(2,1)}, u32[]{:S(2)}) copy-start(bf16[96,1,8,128]{3,2,0,1:T(8,128)(2,1)} %copy-done.30) | copy-start | bytes 589828
  238.0 56.9 %collective-permute-start.1 = (bf16[8,3,32,1024]{3,2,1,0:T(8,128)(2,1)}, bf16[8,3,32,1024]{3,2,1,0:T(8,128)(2,1)}, u32[]{:S(2)}, u32[]{:S(2)}) collective-permute-start(bf16[8,3,32,1024]{3,2,1,0:T(8,128)(2,1)} %broadcast_select_fusion), channel_id=1, source_target_pairs={{0,64},{1,65},{2,66},{3,67},{4,68},{5,69},{6,70},{7,71},{8,72},{9,... | collective-permute-start | bytes 4718600 | tf_op jit(solution)/shard_map/ppermute | solution.py:16
  240.1 4.2 %copy-start.29 = (bf16[96,1,8,128]{3,2,0,1:T(8,128)(2,1)S(1)}, bf16[96,1,8,128]{3,2,0,1:T(8,128)(2,1)}, u32[]{:S(2)}) copy-start(bf16[96,1,8,128]{3,2,0,1:T(8,128)(2,1)} %copy-done.28) | copy-start | bytes 589828
  240.2 4.2 %copy-start.27 = (bf16[96,1,8,128]{3,2,0,1:T(8,128)(2,1)S(1)}, bf16[96,1,8,128]{3,2,0,1:T(8,128)(2,1)}, u32[]{:S(2)}) copy-start(bf16[96,1,8,128]{3,2,0,1:T(8,128)(2,1)} %copy-done.26) | copy-start | bytes 589828
  240.4 4.2 %copy-start.25 = (bf16[96,1,8,128]{3,2,0,1:T(8,128)(2,1)S(1)}, bf16[96,1,8,128]{3,2,0,1:T(8,128)(2,1)}, u32[]{:S(2)}) copy-start(bf16[96,1,8,128]{3,2,0,1:T(8,128)(2,1)} %copy-done.24) | copy-start | bytes 589828
  240.5 4.2 %copy-start.23 = (bf16[96,1,8,128]{3,2,0,1:T(8,128)(2,1)S(1)}, bf16[96,1,8,128]{3,2,0,1:T(8,128)(2,1)}, u32[]{:S(2)}) copy-start(bf16[96,1,8,128]{3,2,0,1:T(8,128)(2,1)} %copy-done.22) | copy-start | bytes 589828
  240.6 4.2 %copy-start.17 = (bf16[96,1,8,128]{3,2,0,1:T(8,128)(2,1)S(1)}, bf16[96,1,8,128]{3,2,0,1:T(8,128)(2,1)}, u32[]{:S(2)}) copy-start(bf16[96,1,8,128]{3,2,0,1:T(8,128)(2,1)} %copy-done.16) | copy-start | bytes 589828
  240.7 4.2 %copy-start.21 = (bf16[96,1,8,128]{3,2,0,1:T(8,128)(2,1)S(1)}, bf16[96,1,8,128]{3,2,0,1:T(8,128)(2,1)}, u32[]{:S(2)}) copy-start(bf16[96,1,8,128]{3,2,0,1:T(8,128)(2,1)} %copy-done.20) | copy-start | bytes 589828
  302.1 2.9 copy-start.61
  (67 other events, 107.0 us)
Sparse Core Ops, SparseCore 0:
  9.0 50.2 all-gather.15
  60.9 39.2 all-gather.13
  101.9 38.0 all-gather.19
  141.5 45.5 all-gather.17
  188.6 42.6 all-gather.23
  232.7 43.8 all-gather.21
where the time goes:
time: 342 us; the launch traced here: 336 us
  waiting for transfers between devices  73.5 us (21%)
  local copies, waits for them, and re-layouts  70.8 us (21%)
  blocking collectives  65 us (19%)
  matrix products  52.3 us (15%)
  other arithmetic  40.9 us (12%)
  starting transfers between devices  17.4 us (5%)
  between operations  16.2 us (5%)
    ppermute x2, waiting for transfers between devices, shifted(): return lax.ppermute(block, axis, route)  60.2 us
    all_gather x1, blocking collectives, local(): lax.all_gather(owners, 'ctx', axis=1, tiled=True)  36.9 us
    dot_general x24, matrix products, attend_rows(): jnp.einsum('tkgj,jkd->tkgd', weights, value_heads, preferred_element_type...  30.3 us
    all_gather x1, blocking collectives, local(): lax.all_gather(doc_start, 'ctx', axis=1, tiled=True)  28.1 us
    unnamed x269, local copies, waits for them, and re-layouts  23.5 us
    dot_general x24, matrix products, attend_rows(): jnp.einsum('tkgd,jkd->tkgj', heads_for_query, heads_for_key, preferred_el...  19.3 us
    reduce_sum x24, other arithmetic, attend_rows(): denom_sum = jnp.sum(exp_terms, axis=-1)  18 us
    all_to_all x3, starting transfers between devices, local(): lax.all_to_all(outgoing, 'ctx', split_axis=0, concat_axis=0, tiled=True)  14.5 us
  transfers between devices with their start and end apart: 11, of which 3 were waited for; matrix products, arithmetic and copies ran while one was open for 40% of the time, Pallas kernels for 0%

commit v1 on v0

v1 whole, which is shorter than its diff:
```python
import functools
import math

import jax
import jax.numpy as jnp
from jax import lax
from jax.experimental import pallas as pl
from jax.experimental.pallas import tpu as pltpu
from jax.sharding import PartitionSpec as P

HEAD_WIDTH = 128
TRACTS_DEV = 16
CH = 32
CAP = 3
DOCMAX = 256
BLOCK = 128
SPAN = BLOCK + DOCMAX
Z = 4
MESH = pl.DeviceIdType.MESH
MASKED = -1e30


def kernel(
    q_hbm,
    k_hbm,
    v_hbm,
    starts_ref,
    owners_ref,
    out_ref,
    q_buf,
    c_buf,
    a_buf,
    b_buf,
    s_buf,
    k_win,
    v_win,
    bias,
    pick,
    dest,
    q_sem,
    kv_sem,
    halo_send,
    halo_recv,
    dest_sem,
    ex_send,
    ex_recv,
    fw_send,
    fw_recv,
    z_send,
    z_recv,
    own_sem,
):
    pipe = lax.axis_index("pipe")
    ctx = lax.axis_index("ctx")
    ctx_count = lax.axis_size("ctx")
    x_lo = ctx // Z
    z = lax.rem(ctx, Z)
    units, rows, width = q_buf.shape
    micro = k_win.shape[0]
    per_micro = units // micro
    scale = 1.0 / math.sqrt(HEAD_WIDTH)

    beside = {"ctx": (1 - x_lo) * Z + z}
    across = {"pipe": 1 - pipe, "ctx": (1 - x_lo) * Z + z}
    right = {"ctx": lax.rem(ctx + 1, ctx_count)}

    def q_load(u):
        m, g = u // per_micro, lax.rem(u, per_micro)
        return pltpu.make_async_copy(
            q_hbm.at[0, m, :, pl.ds(pl.multiple_of(g * width, width), width)],
            q_buf.at[u],
            q_sem.at[u],
        )

    def kv_load(m, which):
        src, dst = ((k_hbm, k_win), (v_hbm, v_win))[which]
        return pltpu.make_async_copy(
            src.at[0, m], dst.at[m, pl.ds(DOCMAX, rows)], kv_sem.at[m, which]
        )

    def halo(m, which):
        src, dst = ((k_hbm, k_win), (v_hbm, v_win))[which]
        return pltpu.make_async_remote_copy(
            src_ref=src.at[0, m, pl.ds(rows - DOCMAX, DOCMAX)],
            dst_ref=dst.at[m, pl.ds(0, DOCMAX)],
            send_sem=halo_send.at[m, which],
            recv_sem=halo_recv.at[m, which],
            device_id=right,
            device_id_type=MESH,
        )

    def dest_copy():
        return pltpu.make_async_remote_copy(
            src_ref=dest.at[0],
            dst_ref=dest.at[1],
            send_sem=dest_sem.at[0],
            recv_sem=dest_sem.at[1],
            device_id=beside,
            device_id_type=MESH,
        )

    def exchange(u):
        return pltpu.make_async_remote_copy(
            src_ref=a_buf.at[u],
            dst_ref=b_buf.at[u],
            send_sem=ex_send.at[u],
            recv_sem=ex_recv.at[u],
            device_id=beside,
            device_id_type=MESH,
        )

    def forward(u):
        return pltpu.make_async_remote_copy(
            src_ref=b_buf.at[u],
            dst_ref=c_buf.at[u],
            send_sem=fw_send.at[u],
            recv_sem=fw_recv.at[u],
            device_id=across,
            device_id_type=MESH,
        )

    def out_slice(u, z_source):
        m, g = u // per_micro, lax.rem(u, per_micro)
        return out_ref.at[
            m, :, z_source, :, :, pl.ds(pl.multiple_of(g * width, width), width)
        ]

    def spread(u, z_to, z_from):
        return pltpu.make_async_remote_copy(
            src_ref=s_buf.at[u, :, z_to],
            dst_ref=out_slice(u, z_from),
            send_sem=z_send.at[u, z_to],
            recv_sem=z_recv.at[u, z_from],
            device_id={"ctx": x_lo * Z + z_to},
            device_id_type=MESH,
        )

    def keep(u):
        return pltpu.make_async_copy(
            s_buf.at[u, :, z], out_slice(u, z), own_sem.at[u]
        )

    for m in range(micro):
        for which in range(2):
            kv_load(m, which).start()

    @pl.loop(0, units)
    def _(u):
        q_load(u).start()

    barrier = pltpu.get_barrier_semaphore()
    for step in range(1, 2 * Z):
        pl.semaphore_signal(
            barrier,
            inc=1,
            device_id={"ctx": lax.rem(ctx + step, 2 * Z)},
            device_id_type=MESH,
        )
    pl.semaphore_signal(barrier, inc=1, device_id=across, device_id_type=MESH)
    pl.semaphore_wait(barrier, 2 * Z)

    for m in range(micro):
        for which in range(2):
            halo(m, which).start()

    lane = lax.broadcasted_iota(jnp.int32, (8, rows), 1)
    sub = lax.broadcasted_iota(jnp.int32, (8, rows), 0)
    tract = lax.shift_right_logical(lane, 5)
    slot = jnp.zeros((8, rows), jnp.int32)
    for m in range(micro):
        names = [owners_ref[m, t] for t in range(TRACTS_DEV)]
        for t in range(TRACTS_DEV):
            rank = jnp.int32(0)
            for earlier in range(t):
                rank = rank + jnp.where(names[earlier] == names[t], 1, 0)
            here = (tract == t) & (sub == m)
            slot = jnp.where(here, names[t] * CAP + rank, slot)
    dest[0] = slot * CH + (lane & (CH - 1))
    dest_copy().start()

    row_at = lax.broadcasted_iota(jnp.int32, (BLOCK, BLOCK), 0)
    col_at = lax.broadcasted_iota(jnp.int32, (BLOCK, BLOCK), 1)
    for m in range(micro):
        for b in range(rows // BLOCK):
            line = starts_ref[pl.ds(m, 1), pl.ds(b * BLOCK, BLOCK)].astype(jnp.float32)
            column = jnp.transpose(jnp.broadcast_to(line, (BLOCK, BLOCK))).astype(jnp.int32)
            first = column - (ctx * rows + b * BLOCK - DOCMAX)
            for part in range(SPAN // BLOCK):
                key_at = col_at + part * BLOCK
                allowed = (key_at >= first) & (key_at <= row_at + DOCMAX)
                bias[m, pl.ds(b * BLOCK, BLOCK), pl.ds(part * BLOCK, BLOCK)] = jnp.where(
                    allowed, 0.0, MASKED
                )

    def pick_rows(m, whose):
        target = dest[whose, pl.ds(m, 1), :] - x_lo * (Z * CAP * CH)
        slots = Z * CAP * CH
        wanted = lax.broadcasted_iota(jnp.int32, (slots, rows), 0)
        pick[m, whose] = jnp.where(wanted == target, 1.0, 0.0).astype(jnp.bfloat16)

    for m in range(micro):
        pick_rows(m, 0)
    dest_copy().wait()
    for m in range(micro):
        pick_rows(m, 1)

    def produce(u):
        m = u // per_micro
        q_load(u).wait()

        @pl.when(lax.rem(u, per_micro) == 0)
        def _():
            for which in range(2):
                kv_load(m, which).wait()
                halo(m, which).wait()

        @pl.when(pipe == 1)
        def _():
            forward(u).wait_recv()
            q_buf[u] = (
                q_buf[u].astype(jnp.float32) + c_buf[u].astype(jnp.float32)
            ).astype(jnp.bfloat16)

        for b in range(rows // BLOCK):
            keys = k_win[m, pl.ds(b * BLOCK, SPAN), :]
            vals = v_win[m, pl.ds(b * BLOCK, SPAN), :]
            for h in range(width // HEAD_WIDTH):
                q = q_buf[u, pl.ds(b * BLOCK, BLOCK), pl.ds(h * HEAD_WIDTH, HEAD_WIDTH)]
                scores = lax.dot_general(
                    q, keys, (((1,), (1,)), ((), ())), preferred_element_type=jnp.float32
                )
                scores = scores + bias[m, pl.ds(b * BLOCK, BLOCK), :]
                top = jnp.max(scores, axis=1, keepdims=True)
                terms = jnp.exp((scores - top) * scale)
                denom = jnp.sum(terms, axis=1, keepdims=True)
                mixed = jnp.dot(
                    terms.astype(jnp.bfloat16), vals, preferred_element_type=jnp.float32
                )
                a_buf[u, pl.ds(b * BLOCK, BLOCK), pl.ds(h * HEAD_WIDTH, HEAD_WIDTH)] = (
                    mixed / denom
                ).astype(jnp.bfloat16)
        exchange(u).start()

    def consume(u):
        m = u // per_micro
        exchange(u).wait_recv()

        @pl.when(pipe == 0)
        def _():
            forward(u).start()

        for whose, source in ((0, a_buf), (1, b_buf)):
            picked = jnp.dot(pick[m, whose], source[u], preferred_element_type=jnp.float32)
            place = x_lo if whose == 0 else 1 - x_lo
            s_buf[u, place] = picked.astype(jnp.bfloat16).reshape(Z, CAP, CH, width)
        for step in (2, 1, 3):
            spread(u, lax.rem(z + step, Z), z).start()
        keep(u).start()

    @pl.loop(0, units + 1)
    def _(step):
        @pl.when(step < units)
        def _():
            produce(step)

        @pl.when(step >= 1)
        def _():
            consume(step - 1)

    @pl.loop(0, units)
    def _(u):
        exchange(u).wait_send()

        @pl.when(pipe == 0)
        def _():
            forward(u).wait_send()

        keep(u).wait()
        for step in range(1, Z):
            other = lax.rem(z + step, Z)
            spread(u, other, z).wait_send()
            spread(u, z, other).wait_recv()


def local(queries, keys, values, doc_start, owners):
    _, micro, rows, width_q = queries.shape
    unit_width = HEAD_WIDTH
    units = micro * (width_q // unit_width)
    bf16, f32, i32 = jnp.bfloat16, jnp.float32, jnp.int32
    dma = pltpu.SemaphoreType.DMA
    anywhere = pl.BlockSpec(memory_space=pl.ANY)
    out = pl.pallas_call(
        kernel,
        out_shape=jax.ShapeDtypeStruct((micro, 2, Z, CAP, CH, width_q), bf16),
        in_specs=[
            anywhere,
            anywhere,
            anywhere,
            pl.BlockSpec(memory_space=pltpu.VMEM),
            pl.BlockSpec(memory_space=pltpu.SMEM),
        ],
        out_specs=anywhere,
        scratch_shapes=[
            pltpu.VMEM((units, rows, unit_width), bf16),
            pltpu.VMEM((units, rows, unit_width), bf16),
            pltpu.VMEM((units, rows, unit_width), bf16),
            pltpu.VMEM((units, rows, unit_width), bf16),
            pltpu.VMEM((units, 2, Z, CAP, CH, unit_width), bf16),
            pltpu.VMEM((micro, DOCMAX + rows, HEAD_WIDTH), bf16),
            pltpu.VMEM((micro, DOCMAX + rows, HEAD_WIDTH), bf16),
            pltpu.VMEM((micro, rows, SPAN), f32),
            pltpu.VMEM((micro, 2, Z * CAP * CH, rows), bf16),
            pltpu.VMEM((2, 8, rows), i32),
            dma((units,)),
            dma((micro, 2)),
            dma((micro, 2)),
            dma((micro, 2)),
            dma((2,)),
            dma((units,)),
            dma((units,)),
            dma((units,)),
            dma((units,)),
            dma((units, Z)),
            dma((units, Z)),
            dma((units,)),
        ],
        compiler_params=pltpu.CompilerParams(
            collective_id=0, has_side_effects=True, vmem_limit_bytes=48 * 1024 * 1024
        ),
    )(queries, keys, values, doc_start, owners)
    return out.reshape(1, micro, 1, 2 * Z, CAP, CH, width_q)


def solution(mesh):
    return jax.shard_map(
        local,
        mesh=mesh,
        in_specs=(
            P("pipe", None, "ctx", "tp"),
            P("pipe", None, "ctx", "tp"),
            P("pipe", None, "ctx", "tp"),
            P(None, "ctx"),
            P(None, "ctx"),
        ),
        out_specs=P("pipe", None, "ctx", None, None, None, "tp"),
        check_vma=False,
    )
```

time: 342 us -> 90.1 us (0.26); the launches traced: 336 us -> 89.9 us
  Pallas kernels: 0 us -> 83.3 us
  waiting for transfers between devices: 73.5 us -> 0 us
  blocking collectives: 65 us -> 0 us
  local copies, waits for them, and re-layouts: 70.8 us -> 6.52 us
  matrix products: 52.3 us -> 0 us
  other arithmetic: 40.9 us -> 0 us
  starting transfers between devices: 17.4 us -> 0 us
  between operations: 16.2 us -> 0.01 us
    pallas_call x0 -> x1, Pallas kernels: none -> 83.3 us  [local(): pl.pallas_call(kernel, out_shape=jax.ShapeDtypeStruct((micro, 2, Z, CAP,...]
    all_gather x2 -> x0, blocking collectives: 65 us -> none  [the longest x1 36.9 us: local(): lax.all_gather(owners, 'ctx', axis=1, tiled=True)]
    ppermute x2 -> x0, waiting for transfers between devices: 60.2 us -> none  [shifted(): return lax.ppermute(block, axis, route)]
    dot_general x51 -> x0, matrix products: 52.3 us -> none  [the longest x24 30.3 us: attend_rows(): jnp.einsum('tkgj,jkd->tkgd', weights, value_heads, preferred_element_type...]
    reduce_sum x30 -> x0, other arithmetic: 19.9 us -> none  [the longest x24 18 us: attend_rows(): denom_sum = jnp.sum(exp_terms, axis=-1)]
    unnamed x269 -> x11, local copies, waits for them, and re-layouts: 23.5 us -> 6.52 us
    convert_element_type x43 -> x0, local copies, waits for them, and re-layouts: 15.7 us -> none  [the longest x40 9.64 us: attend_rows(): return attended.reshape(query_count, -1).astype(jnp.bfloat16)]
    all_to_all x3 -> x0, starting transfers between devices: 14.5 us -> none  [local(): lax.all_to_all(outgoing, 'ctx', split_axis=0, concat_axis=0, tiled=True)]
  transfers between devices with their start and end apart: 11 -> 0, of which waited for: 3 -> 0; matrix products, arithmetic and copies ran while one was open for 40% -> 0% of each run, Pallas kernels for 0% -> 0%
where the time goes in v1:
time: 90.1 us; the launch traced here: 89.9 us
  Pallas kernels  83.3 us (92%)
  local copies, waits for them, and re-layouts  6.52 us (7%)
    pallas_call x1, Pallas kernels, local(): pl.pallas_call(kernel, out_shape=jax.ShapeDtypeStruct((micro, 2, Z, CAP,...  83.3 us
    unnamed x11, local copies, waits for them, and re-layouts  6.52 us

profile of v1, /device:TPU:20, one launch (start us, length us, event | category | flops | bytes accessed | tf_op | source)
XLA Modules:
  0.0 89.9 jit_solution(14236991292531942145)
XLA Ops:
  0.0 0.0 copy-start
  0.0 1.6 %copy-done = bf16[1,2,512,1024]{3,2,1,0:T(8,128)(2,1)S(1)} copy-done((bf16[1,2,512,1024]{3,2,1,0:T(8,128)(2,1)S(1)}, bf16[1,2,512,1024]{3,2,1,0:T(8,128)(2,1)}, u32[]{:S(2)}) %copy-start) | copy-done | bytes 2097176
  1.6 0.0 copy-start.1
  1.6 0.9 %copy-done.1 = bf16[1,2,512,128]{3,2,1,0:T(8,128)(2,1)S(1)} copy-done((bf16[1,2,512,128]{3,2,1,0:T(8,128)(2,1)S(1)}, bf16[1,2,512,128]{3,2,1,0:T(8,128)(2,1)}, u32[]{:S(2)}) %copy-start.1) | copy-done | bytes 262168
  2.5 0.0 copy-start.2
  2.5 0.9 %copy-done.2 = bf16[1,2,512,128]{3,2,1,0:T(8,128)(2,1)S(1)} copy-done((bf16[1,2,512,128]{3,2,1,0:T(8,128)(2,1)S(1)}, bf16[1,2,512,128]{3,2,1,0:T(8,128)(2,1)}, u32[]{:S(2)}) %copy-start.2) | copy-done | bytes 262168
  3.5 0.0 copy-start.3
  3.5 0.7 copy-done.3
  4.2 0.0 copy-start.4
  4.2 0.7 copy-done.4
  4.9 83.3 %shard_map.55 = bf16[2,2,4,3,32,1024]{5,4,3,2,1,0:T(8,128)(2,1)S(1)} custom-call(bf16[1,2,512,1024]{3,2,1,0:T(8,128)(2,1)S(1)} %copy-done, bf16[1,2,512,128]{3,2,1,0:T(8,128)(2,1)S(1)} %copy-done.1, bf16[1,2,512,128]{3,2,1,0:T(8,128)(2,1)S(1)} %copy-done.2, s32[2,512]{1,0:T(2,128)S(1)} %copy-done.3, s32[2,16]{1,0:T(2,128)S(1)} %copy-done.4), custom_call_target="tpu_custom_call" | custom-call | tf_op jit(solution)/shard_map/pallas_call | solution.py:292
  88.2 1.7 %copy.8 = bf16[1,2,1,8,3,32,1024]{6,5,4,3,2,1,0:T(8,128)(2,1)} copy(bf16[1,2,1,8,3,32,1024]{6,5,4,3,2,1,0:T(8,128)(2,1)S(1)} %bitcast.3) | data formatting | bytes 6291456
Async XLA Ops:
  0.0 1.6 %copy-start = (bf16[1,2,512,1024]{3,2,1,0:T(8,128)(2,1)S(1)}, bf16[1,2,512,1024]{3,2,1,0:T(8,128)(2,1)}, u32[]{:S(2)}) copy-start(bf16[1,2,512,1024]{3,2,1,0:T(8,128)(2,1)} %q_hbm.1) | copy-start | bytes 6291460
  1.6 0.9 %copy-start.1 = (bf16[1,2,512,128]{3,2,1,0:T(8,128)(2,1)S(1)}, bf16[1,2,512,128]{3,2,1,0:T(8,128)(2,1)}, u32[]{:S(2)}) copy-start(bf16[1,2,512,128]{3,2,1,0:T(8,128)(2,1)} %k_hbm.1) | copy-start | bytes 786436
  2.5 0.9 %copy-start.2 = (bf16[1,2,512,128]{3,2,1,0:T(8,128)(2,1)S(1)}, bf16[1,2,512,128]{3,2,1,0:T(8,128)(2,1)}, u32[]{:S(2)}) copy-start(bf16[1,2,512,128]{3,2,1,0:T(8,128)(2,1)} %v_hbm.1) | copy-start | bytes 786436
  3.5 0.7 copy-start.3
  4.2 0.7 copy-start.4

commit v2 on v1

v2 whole, which is shorter than its diff:
```python
import functools
import math

import jax
import jax.numpy as jnp
from jax import lax
from jax.experimental import pallas as pl
from jax.experimental.pallas import tpu as pltpu
from jax.sharding import PartitionSpec as P

HEAD_WIDTH = 128
TRACTS_DEV = 16
CH = 32
CAP = 3
DOCMAX = 256
BLOCK = 128
SPAN = BLOCK + DOCMAX
CHUNK = 256
LAG = 6
Z = 4
MESH = pl.DeviceIdType.MESH
MASKED = -1e30


def kernel(
    q_hbm,
    k_hbm,
    v_hbm,
    starts_hbm,
    owners_hbm,
    out_ref,
    q_buf,
    c_buf,
    a_buf,
    b_buf,
    s_buf,
    k_win,
    v_win,
    bias,
    pick,
    dest,
    starts_ref,
    owners_ref,
    small_sem,
    q_sem,
    kv_sem,
    halo_send,
    halo_recv,
    dest_sem,
    ex_send,
    ex_recv,
    fw_send,
    fw_recv,
    to_send,
    to_recv,
    own_sem,
):
    pipe = lax.axis_index("pipe")
    ctx = lax.axis_index("ctx")
    ctx_count = lax.axis_size("ctx")
    x_lo = ctx // Z
    z = lax.rem(ctx, Z)
    units, rows, width = q_buf.shape
    micro = k_win.shape[0]
    per_micro = units // micro
    chunks = rows // CHUNK
    half = chunks // 2
    steps = units * chunks
    slots = Z * CAP * CH
    scale = math.log2(math.e) / math.sqrt(HEAD_WIDTH)

    beside = {"ctx": (1 - x_lo) * Z + z}
    across = {"pipe": 1 - pipe, "ctx": (1 - x_lo) * Z + z}
    right = {"ctx": lax.rem(ctx + 1, ctx_count)}

    def chunk_at(step):
        return (
            step
            + jnp.where(step // half == 1, half, 0)
            - jnp.where(step // half == 2, half, 0)
        )

    def first_row(chunk):
        part = lax.rem(lax.rem(chunk, chunks) + half, chunks)
        return pl.multiple_of(part * CHUNK, CHUNK)

    def columns(u):
        return pl.ds(pl.multiple_of(lax.rem(u, per_micro) * width, width), width)

    def q_load(u):
        return pltpu.make_async_copy(
            q_hbm.at[0, u // per_micro, :, columns(u)], q_buf.at[u], q_sem.at[u]
        )

    def starts_load():
        return pltpu.make_async_copy(starts_hbm, starts_ref, small_sem.at[0])

    def owners_load():
        return pltpu.make_async_copy(owners_hbm, owners_ref, small_sem.at[1])

    def kv_load(m, which):
        src, dst = ((k_hbm, k_win), (v_hbm, v_win))[which]
        return pltpu.make_async_copy(
            src.at[0, m], dst.at[m, pl.ds(DOCMAX, rows)], kv_sem.at[m, which]
        )

    def halo(m, which):
        src, dst = ((k_hbm, k_win), (v_hbm, v_win))[which]
        return pltpu.make_async_remote_copy(
            src_ref=src.at[0, m, pl.ds(rows - DOCMAX, DOCMAX)],
            dst_ref=dst.at[m, pl.ds(0, DOCMAX)],
            send_sem=halo_send.at[m, which],
            recv_sem=halo_recv.at[m, which],
            device_id=right,
            device_id_type=MESH,
        )

    def dest_copy():
        return pltpu.make_async_remote_copy(
            src_ref=dest.at[0],
            dst_ref=dest.at[1],
            send_sem=dest_sem.at[0],
            recv_sem=dest_sem.at[1],
            device_id=beside,
            device_id_type=MESH,
        )

    def exchange(chunk):
        u, span = chunk // chunks, pl.ds(first_row(chunk), CHUNK)
        return pltpu.make_async_remote_copy(
            src_ref=a_buf.at[u, span],
            dst_ref=b_buf.at[u, span],
            send_sem=ex_send.at[chunk],
            recv_sem=ex_recv.at[chunk],
            device_id=beside,
            device_id_type=MESH,
        )

    def forward(chunk):
        u, span = chunk // chunks, pl.ds(first_row(chunk), CHUNK)
        return pltpu.make_async_remote_copy(
            src_ref=b_buf.at[u, span],
            dst_ref=c_buf.at[u, span],
            send_sem=fw_send.at[chunk],
            recv_sem=fw_recv.at[chunk],
            device_id=across,
            device_id_type=MESH,
        )

    def spread_near(u, z_to, z_from):
        return pltpu.make_async_remote_copy(
            src_ref=s_buf.at[u, :, z_to],
            dst_ref=out_ref.at[u // per_micro, :, z_from, :, :, columns(u)],
            send_sem=to_send.at[u, z_to],
            recv_sem=to_recv.at[u, z_from],
            device_id={"ctx": x_lo * Z + z_to},
            device_id_type=MESH,
        )

    def keep_near(u):
        return pltpu.make_async_copy(
            s_buf.at[u, :, z],
            out_ref.at[u // per_micro, :, z, :, :, columns(u)],
            own_sem.at[u],
        )

    def spread_far(u, to, source):
        return pltpu.make_async_remote_copy(
            src_ref=s_buf.at[u, to // Z, lax.rem(to, Z)],
            dst_ref=out_ref.at[
                u // per_micro, source // Z, lax.rem(source, Z), :, :, columns(u)
            ],
            send_sem=to_send.at[u, to],
            recv_sem=to_recv.at[u, source],
            device_id={"ctx": to},
            device_id_type=MESH,
        )

    def keep_far(u):
        return pltpu.make_async_copy(
            s_buf.at[u, x_lo, z],
            out_ref.at[u // per_micro, x_lo, z, :, :, columns(u)],
            own_sem.at[u],
        )

    starts_load().start()
    for which in range(2):
        kv_load(0, which).start()
    q_load(0).start()
    q_load(1).start()
    owners_load().start()
    for which in range(2):
        kv_load(1, which).start()

    @pl.loop(2, units)
    def _(u):
        q_load(u).start()

    barrier = pltpu.get_barrier_semaphore()
    for step in range(1, 2 * Z):
        pl.semaphore_signal(
            barrier,
            inc=1,
            device_id={"ctx": lax.rem(ctx + step, 2 * Z)},
            device_id_type=MESH,
        )
    pl.semaphore_signal(barrier, inc=1, device_id=across, device_id_type=MESH)

    def mask_rows(m):
        row_at = lax.broadcasted_iota(jnp.int32, (BLOCK, BLOCK), 0)
        col_at = lax.broadcasted_iota(jnp.int32, (BLOCK, BLOCK), 1)
        for b in range(rows // BLOCK):
            line = starts_ref[pl.ds(m, 1), pl.ds(b * BLOCK, BLOCK)].astype(jnp.float32)
            column = jnp.transpose(jnp.broadcast_to(line, (BLOCK, BLOCK))).astype(jnp.int32)
            first = column - (ctx * rows + b * BLOCK - DOCMAX)
            for part in range(SPAN // BLOCK):
                key_at = col_at + part * BLOCK
                allowed = (key_at >= first) & (key_at <= row_at + DOCMAX)
                bias[m, pl.ds(b * BLOCK, BLOCK), pl.ds(part * BLOCK, BLOCK)] = jnp.where(
                    allowed, 0.0, MASKED
                )

    def find_dest():
        owners_load().wait()
        lane = lax.broadcasted_iota(jnp.int32, (8, rows), 1)
        sub = lax.broadcasted_iota(jnp.int32, (8, rows), 0)
        tract = lax.shift_right_logical(lane, 5)
        slot = jnp.zeros((8, rows), jnp.int32)
        for m in range(micro):
            names = [owners_ref[m, t] for t in range(TRACTS_DEV)]
            for t in range(TRACTS_DEV):
                rank = jnp.int32(0)
                for earlier in range(t):
                    rank = rank + jnp.where(names[earlier] == names[t], 1, 0)
                here = (tract == t) & (sub == m)
                slot = jnp.where(here, names[t] * CAP + rank, slot)
        dest[0] = slot * CH + (lane & (CH - 1))

    def pick_rows(m, whose, at, first, count):
        target = dest[whose, pl.ds(m, 1), :] - first
        wanted = lax.broadcasted_iota(jnp.int32, (count, rows), 0)
        pick[m, pl.ds(at, count), :] = jnp.where(wanted == target, 1.0, 0.0).astype(
            jnp.bfloat16
        )

    def attend(chunk):
        u = chunk // chunks
        m = u // per_micro
        base = first_row(chunk)
        for b in range(CHUNK // BLOCK):
            span = pl.ds(base + b * BLOCK, BLOCK)
            keys = k_win[m, pl.ds(base + b * BLOCK, SPAN), :]
            vals = v_win[m, pl.ds(base + b * BLOCK, SPAN), :]
            scores = lax.dot_general(
                q_buf[u, span, :],
                keys,
                (((1,), (1,)), ((), ())),
                preferred_element_type=jnp.float32,
            )
            scores = scores + bias[m, span, :]
            top = jnp.max(scores, axis=1, keepdims=True)
            terms = jnp.exp2((scores - top) * scale)
            denom = jnp.sum(terms, axis=1, keepdims=True)
            mixed = jnp.dot(
                terms.astype(jnp.bfloat16), vals, preferred_element_type=jnp.float32
            )
            a_buf[u, span, :] = (mixed / denom).astype(jnp.bfloat16)

    def await_inputs(chunk):
        u, part = chunk // chunks, lax.rem(chunk, chunks)
        m, g = u // per_micro, lax.rem(u, per_micro)

        @pl.when(part == 0)
        def _():
            q_load(u).wait()

        @pl.when((part == 0) & (g == 0))
        def _():
            for which in range(2):
                kv_load(m, which).wait()

        @pl.when((part == half) & (g == 0))
        def _():
            for which in range(2):
                halo(m, which).wait_recv()

    starts_load().wait()
    mask_rows(0)
    pl.semaphore_wait(barrier, 2 * Z)
    for which in range(2):
        halo(0, which).start()

    @pl.when(pipe == 0)
    def _():
        @pl.loop(0, steps + LAG)
        def _(step):
            @pl.when(step < steps)
            def _():
                chunk = chunk_at(step)
                await_inputs(chunk)
                attend(chunk)
                exchange(chunk).start()

            @pl.when(step >= LAG)
            def _():
                chunk = chunk_at(step - LAG)
                u = chunk // chunks
                m = u // per_micro
                exchange(chunk).wait_recv()
                forward(chunk).start()

                @pl.when(lax.rem(chunk, chunks) == chunks - 1)
                def _():
                    for place, source, first in (
                        (x_lo, a_buf, 0),
                        (1 - x_lo, b_buf, slots),
                    ):
                        picked = jnp.dot(
                            pick[m, pl.ds(first, slots), :],
                            source[u],
                            preferred_element_type=jnp.float32,
                        )
                        s_buf[u, place] = picked.astype(jnp.bfloat16).reshape(
                            Z, CAP, CH, width
                        )
                    for turn in (2, 1, 3):
                        spread_near(u, lax.rem(z + turn, Z), z).start()
                    keep_near(u).start()

            @pl.when(step == 0)
            def _():
                find_dest()
                dest_copy().start()
                pick_rows(0, 0, 0, x_lo * slots, slots)

            @pl.when(step == half)
            def _():
                dest_copy().wait()
                pick_rows(0, 1, slots, x_lo * slots, slots)

            @pl.when(step == 4 * chunks)
            def _():
                for which in range(2):
                    halo(1, which).start()
                mask_rows(1)

            @pl.when(step == 5 * chunks)
            def _():
                pick_rows(1, 0, 0, x_lo * slots, slots)

            @pl.when(step == 6 * chunks)
            def _():
                pick_rows(1, 1, slots, x_lo * slots, slots)

        @pl.loop(0, steps)
        def _(chunk):
            exchange(chunk).wait_send()
            forward(chunk).wait_send()

        @pl.loop(0, units)
        def _(u):
            keep_near(u).wait()
            for turn in range(1, Z):
                other = lax.rem(z + turn, Z)
                spread_near(u, other, z).wait_send()
                spread_near(u, z, other).wait_recv()

    @pl.when(pipe == 1)
    def _():
        find_dest()
        for m in range(micro):
            pick_rows(m, 0, 0, 0, 2 * slots)
        mask_rows(1)

        @pl.loop(0, steps)
        def _(step):
            chunk = chunk_at(step)
            u = chunk // chunks
            m = u // per_micro
            span = pl.ds(first_row(chunk), CHUNK)
            @pl.when(step == 4 * chunks)
            def _():
                for which in range(2):
                    halo(1, which).start()
            await_inputs(chunk)
            forward(chunk).wait_recv()
            q_buf[u, span, :] = (
                q_buf[u, span, :].astype(jnp.float32) + c_buf[u, span, :].astype(jnp.float32)
            ).astype(jnp.bfloat16)
            attend(chunk)

            @pl.when(lax.rem(chunk, chunks) == chunks - 1)
            def _():
                picked = jnp.dot(pick[m], a_buf[u], preferred_element_type=jnp.float32)
                s_buf[u] = picked.astype(jnp.bfloat16).reshape(2, Z, CAP, CH, width)
                for turn in (6, 2, 5, 7, 4, 1, 3):
                    spread_far(u, lax.rem(ctx + turn, 2 * Z), ctx).start()
                keep_far(u).start()

        @pl.loop(0, units)
        def _(u):
            keep_far(u).wait()
            for turn in range(1, 2 * Z):
                other = lax.rem(ctx + turn, 2 * Z)
                spread_far(u, other, ctx).wait_send()
                spread_far(u, ctx, other).wait_recv()

    for m in range(micro):
        for which in range(2):
            halo(m, which).wait_send()


def local(queries, keys, values, doc_start, owners):
    _, micro, rows, width_q = queries.shape
    unit_width = HEAD_WIDTH
    units = micro * (width_q // unit_width)
    steps = units * (rows // CHUNK)
    bf16, f32, i32 = jnp.bfloat16, jnp.float32, jnp.int32
    dma = pltpu.SemaphoreType.DMA
    in_hbm = pl.BlockSpec(memory_space=pltpu.HBM)
    out = pl.pallas_call(
        kernel,
        out_shape=jax.ShapeDtypeStruct((micro, 2, Z, CAP, CH, width_q), bf16),
        in_specs=[in_hbm] * 5,
        out_specs=pl.BlockSpec(memory_space=pl.ANY),
        scratch_shapes=[
            pltpu.VMEM((units, rows, unit_width), bf16),
            pltpu.VMEM((units, rows, unit_width), bf16),
            pltpu.VMEM((units, rows, unit_width), bf16),
            pltpu.VMEM((units, rows, unit_width), bf16),
            pltpu.VMEM((units, 2, Z, CAP, CH, unit_width), bf16),
            pltpu.VMEM((micro, DOCMAX + rows, HEAD_WIDTH), bf16),
            pltpu.VMEM((micro, DOCMAX + rows, HEAD_WIDTH), bf16),
            pltpu.VMEM((micro, rows, SPAN), f32),
            pltpu.VMEM((micro, 2 * Z * CAP * CH, rows), bf16),
            pltpu.VMEM((2, 8, rows), i32),
            pltpu.VMEM((micro, rows), i32),
            pltpu.SMEM((micro, TRACTS_DEV), i32),
            dma((2,)),
            dma((units,)),
            dma((micro, 2)),
            dma((micro, 2)),
            dma((micro, 2)),
            dma((2,)),
            dma((steps,)),
            dma((steps,)),
            dma((steps,)),
            dma((steps,)),
            dma((units, 2 * Z)),
            dma((units, 2 * Z)),
            dma((units,)),
        ],
        compiler_params=pltpu.CompilerParams(
            collective_id=0, has_side_effects=True, vmem_limit_bytes=48 * 1024 * 1024
        ),
    )(*[pltpu.with_memory_space_constraint(a, pltpu.HBM) for a in (queries, keys, values, doc_start, owners)])
    return out.reshape(1, micro, 1, 2 * Z, CAP, CH, width_q)


def solution(mesh):
    return jax.shard_map(
        local,
        mesh=mesh,
        in_specs=(
            P("pipe", None, "ctx", "tp"),
            P("pipe", None, "ctx", "tp"),
            P("pipe", None, "ctx", "tp"),
            P(None, "ctx"),
            P(None, "ctx"),
        ),
        out_specs=P("pipe", None, "ctx", None, None, None, "tp"),
        check_vma=False,
    )
```

time: 90.1 us -> 73.2 us (0.81)
  Pallas kernels: 83.3 us -> 71.4 us
  local copies, waits for them, and re-layouts: 6.52 us -> 1.67 us
    pallas_call x1, Pallas kernels: 83.3 us -> 71.4 us  [local(): pl.pallas_call(kernel, out_shape=jax.ShapeDtypeStruct((micro, 2, Z, CAP,...]
    unnamed x11 -> x1, local copies, waits for them, and re-layouts: 6.52 us -> 1.67 us
where the time goes in v2:
time: 73.2 us; the launch traced here: 73.1 us
  Pallas kernels  71.4 us (98%)
  local copies, waits for them, and re-layouts  1.67 us (2%)
    pallas_call x1, Pallas kernels, local(): pl.pallas_call(kernel, out_shape=jax.ShapeDtypeStruct((micro, 2, Z, CAP,...  71.4 us
    unnamed x1, local copies, waits for them, and re-layouts  1.67 us

profile of v2, /device:TPU:20, one launch (start us, length us, event | category | flops | bytes accessed | tf_op | source)
XLA Modules:
  0.0 73.1 jit_solution(10275510734844255537)
XLA Ops:
  0.0 71.4 %shard_map.55 = bf16[2,2,4,3,32,1024]{5,4,3,2,1,0:T(8,128)(2,1)S(1)} custom-call(bf16[1,2,512,1024]{3,2,1,0:T(8,128)(2,1)} %q_hbm.1, bf16[1,2,512,128]{3,2,1,0:T(8,128)(2,1)} %k_hbm.1, bf16[1,2,512,128]{3,2,1,0:T(8,128)(2,1)} %v_hbm.1, s32[2,512]{1,0:T(2,128)} %starts_hbm.1, s32[2,16]{1,0:T(2,128)} %owners_hbm.1), custom_call_target="tpu_custom_call" | custom-call | tf_op jit(solution)/shard_map/pallas_call | solution.py:421
  71.4 1.7 %copy.8 = bf16[1,2,1,8,3,32,1024]{6,5,4,3,2,1,0:T(8,128)(2,1)} copy(bf16[1,2,1,8,3,32,1024]{6,5,4,3,2,1,0:T(8,128)(2,1)S(1)} %bitcast.3) | data formatting | bytes 6291456

commit v3 on v2

v3 whole, which is shorter than its diff:
```python
import functools
import math

import jax
import jax.numpy as jnp
from jax import lax
from jax.experimental import pallas as pl
from jax.experimental.pallas import tpu as pltpu
from jax.sharding import PartitionSpec as P

HEAD_WIDTH = 128
TRACTS_DEV = 16
CH = 32
CAP = 3
DOCMAX = 256
BLOCK = 128
SPAN = BLOCK + DOCMAX
CHUNK = 256
EARLY = 7
FIRST = 2
MORE = 4
Z = 4
MESH = pl.DeviceIdType.MESH
MASKED = -1e30


def kernel(
    q_hbm,
    k_hbm,
    v_hbm,
    starts_hbm,
    owners_hbm,
    out_ref,
    q_buf,
    relay,
    c_buf,
    a_buf,
    b_buf,
    s_buf,
    k_win,
    v_win,
    bias,
    pick,
    dest,
    starts_ref,
    owners_ref,
    small_sem,
    q_sem,
    kv_sem,
    halo_send,
    halo_recv,
    relay_sem,
    dest_sem,
    ex_recv,
    fw_recv,
    all_send,
    all_recv,
):
    pipe = lax.axis_index("pipe")
    ctx = lax.axis_index("ctx")
    ctx_count = lax.axis_size("ctx")
    x_lo = ctx // Z
    z = lax.rem(ctx, Z)
    units, rows, width = q_buf.shape
    micro = k_win.shape[0]
    per_micro = units // micro
    chunks = rows // CHUNK
    steps = units * chunks
    slots = Z * CAP * CH
    scale = math.log2(math.e) / math.sqrt(HEAD_WIDTH)

    beside = {"ctx": (1 - x_lo) * Z + z}
    across = {"pipe": 1 - pipe, "ctx": (1 - x_lo) * Z + z}
    right = {"ctx": lax.rem(ctx + 1, ctx_count)}

    def chunk_at(step):
        return jnp.where(
            step < EARLY,
            2 * step,
            jnp.where(step < 2 * EARLY, 2 * (step - EARLY) + 1, step),
        )

    def first_row(chunk):
        return pl.multiple_of((1 - lax.rem(chunk, chunks)) * CHUNK, CHUNK)

    def columns(u):
        return pl.ds(pl.multiple_of(lax.rem(u, per_micro) * width, width), width)

    def q_load(u):
        return pltpu.make_async_copy(
            q_hbm.at[0, u // per_micro, :, columns(u)], q_buf.at[u], q_sem.at[u]
        )

    def starts_load():
        return pltpu.make_async_copy(starts_hbm, starts_ref, small_sem.at[0])

    def owners_load():
        return pltpu.make_async_copy(owners_hbm, owners_ref, small_sem.at[1])

    def kv_load(m, which):
        src, dst = ((k_hbm, k_win), (v_hbm, v_win))[which]
        return pltpu.make_async_copy(
            src.at[0, m],
            dst.at[m, pl.ds(DOCMAX, rows), pl.ds(0, HEAD_WIDTH)],
            kv_sem.at[m, which],
        )

    def halo_ends(m, which):
        src, dst = ((k_hbm, k_win), (v_hbm, v_win))[which]
        return (
            src.at[0, m, pl.ds(rows - DOCMAX, DOCMAX)],
            dst.at[m, pl.ds(0, DOCMAX), pl.ds(0, HEAD_WIDTH)],
        )

    def halo(m, which):
        src, dst = halo_ends(m, which)
        return pltpu.make_async_remote_copy(
            src_ref=src,
            dst_ref=dst,
            send_sem=halo_send.at[m, which],
            recv_sem=halo_recv.at[m, which],
            device_id=right,
            device_id_type=MESH,
        )

    def relay_z(m, which):
        return (2 * m + which + Z - 1) % Z

    def to_relay(m, which):
        return pltpu.make_async_remote_copy(
            src_ref=halo_ends(m, which)[0],
            dst_ref=relay,
            send_sem=halo_send.at[m, which],
            recv_sem=relay_sem.at[0],
            device_id={"ctx": relay_z(m, which)},
            device_id_type=MESH,
        )

    def from_relay(m, which):
        return pltpu.make_async_remote_copy(
            src_ref=relay,
            dst_ref=halo_ends(m, which)[1],
            send_sem=relay_sem.at[1],
            recv_sem=halo_recv.at[m, which],
            device_id={"ctx": Z},
            device_id_type=MESH,
        )

    def send_halo(m):
        for which in range(2):
            via = relay_z(m, which)
            if via == Z - 1:
                direct = ctx < ctx_count - 1
            else:
                direct = (ctx < ctx_count - 1) & (ctx != Z - 1)

                @pl.when(ctx == Z - 1)
                def _():
                    to_relay(m, which).start()

            @pl.when(direct)
            def _():
                halo(m, which).start()

    def pass_halo(m):
        for which in range(2):
            via = relay_z(m, which)
            if via != Z - 1:

                @pl.when(ctx == via)
                def _():
                    to_relay(m, which).wait_recv()
                    from_relay(m, which).start()

    def dest_copy():
        return pltpu.make_async_remote_copy(
            src_ref=dest.at[0],
            dst_ref=dest.at[1],
            send_sem=dest_sem.at[0],
            recv_sem=dest_sem.at[1],
            device_id=beside,
            device_id_type=MESH,
        )

    def exchange(chunk):
        u, span = chunk // chunks, pl.ds(first_row(chunk), CHUNK)
        return pltpu.make_async_remote_copy(
            src_ref=a_buf.at[u, span],
            dst_ref=b_buf.at[u, span],
            send_sem=all_send.at[0],
            recv_sem=ex_recv.at[chunk],
            device_id=beside,
            device_id_type=MESH,
        )

    def forward(chunk):
        u, span = chunk // chunks, pl.ds(first_row(chunk), CHUNK)
        return pltpu.make_async_remote_copy(
            src_ref=b_buf.at[u, span],
            dst_ref=c_buf.at[u, span],
            send_sem=all_send.at[1],
            recv_sem=fw_recv.at[chunk],
            device_id=across,
            device_id_type=MESH,
        )

    def spread_near(u, z_to, z_from):
        return pltpu.make_async_remote_copy(
            src_ref=s_buf.at[u, :, z_to],
            dst_ref=out_ref.at[u // per_micro, :, z_from, :, :, columns(u)],
            send_sem=all_send.at[2],
            recv_sem=all_recv.at[0],
            device_id={"ctx": x_lo * Z + z_to},
            device_id_type=MESH,
        )

    def keep_near(u):
        return pltpu.make_async_copy(
            s_buf.at[u, :, z],
            out_ref.at[u // per_micro, :, z, :, :, columns(u)],
            all_recv.at[0],
        )

    def spread_far(u, to, source):
        return pltpu.make_async_remote_copy(
            src_ref=s_buf.at[u, to // Z, lax.rem(to, Z)],
            dst_ref=out_ref.at[
                u // per_micro, source // Z, lax.rem(source, Z), :, :, columns(u)
            ],
            send_sem=all_send.at[2],
            recv_sem=all_recv.at[0],
            device_id={"ctx": to},
            device_id_type=MESH,
        )

    def keep_far(u):
        return pltpu.make_async_copy(
            s_buf.at[u, x_lo, z],
            out_ref.at[u // per_micro, x_lo, z, :, :, columns(u)],
            all_recv.at[0],
        )

    barrier = pltpu.get_barrier_semaphore()
    for step in range(1, 2 * Z):
        pl.semaphore_signal(
            barrier,
            inc=1,
            device_id={"ctx": lax.rem(ctx + step, 2 * Z)},
            device_id_type=MESH,
        )
    pl.semaphore_signal(barrier, inc=1, device_id=across, device_id_type=MESH)

    starts_load().start()
    for which in range(2):
        kv_load(0, which).start()
    owners_load().start()

    @pl.loop(0, units)
    def _(u):
        q_load(u).start()

    for which in range(2):
        kv_load(1, which).start()

    def mask_rows(m):
        row_at = lax.broadcasted_iota(jnp.int32, (BLOCK, BLOCK), 0)
        col_at = lax.broadcasted_iota(jnp.int32, (BLOCK, BLOCK), 1)
        for b in range(rows // BLOCK):
            line = starts_ref[pl.ds(m, 1), pl.ds(b * BLOCK, BLOCK)].astype(jnp.float32)
            column = jnp.transpose(jnp.broadcast_to(line, (BLOCK, BLOCK))).astype(jnp.int32)
            first = column - (ctx * rows + b * BLOCK - DOCMAX)
            for part in range(SPAN // BLOCK):
                key_at = col_at + part * BLOCK
                allowed = (key_at >= first) & (key_at <= row_at + DOCMAX)
                bias[m, pl.ds(b * BLOCK, BLOCK), pl.ds(part * BLOCK, BLOCK)] = jnp.where(
                    allowed, 0.0, MASKED
                )

    def find_dest():
        owners_load().wait()
        lane = lax.broadcasted_iota(jnp.int32, (8, rows), 1)
        sub = lax.broadcasted_iota(jnp.int32, (8, rows), 0)
        tract = lax.shift_right_logical(lane, 5)
        slot = jnp.zeros((8, rows), jnp.int32)
        for m in range(micro):
            names = [owners_ref[m, t] for t in range(TRACTS_DEV)]
            for t in range(TRACTS_DEV):
                rank = jnp.int32(0)
                for earlier in range(t):
                    rank = rank + jnp.where(names[earlier] == names[t], 1, 0)
                here = (tract == t) & (sub == m)
                slot = jnp.where(here, names[t] * CAP + rank, slot)
        dest[0] = slot * CH + (lane & (CH - 1))

    def pick_rows(m, whose, at, first, count):
        target = dest[whose, pl.ds(m, 1), :] - first
        wanted = lax.broadcasted_iota(jnp.int32, (count, rows), 0)
        pick[m, pl.ds(at, count), :] = jnp.where(wanted == target, 1.0, 0.0).astype(
            jnp.bfloat16
        )

    def attend(chunk, section):
        u = chunk // chunks
        m = u // per_micro
        base = first_row(chunk)
        spans = [pl.ds(base + b * BLOCK, BLOCK) for b in range(CHUNK // BLOCK)]
        windows = [pl.ds(base + b * BLOCK, SPAN) for b in range(CHUNK // BLOCK)]
        terms = []
        for span, window in zip(spans, windows):
            q = q_buf[u, span, :]
            if section:
                q = (q.astype(jnp.float32) + c_buf[u, span, :].astype(jnp.float32)).astype(
                    jnp.bfloat16
                )
            scores = lax.dot_general(
                q, k_win[m, window, :], (((1,), (1,)), ((), ())), preferred_element_type=jnp.float32
            )
            scores = scores + bias[m, span, :]
            top = jnp.max(scores, axis=1, keepdims=True)
            terms.append(jnp.exp2((scores - top) * scale).astype(jnp.bfloat16))
        for span, window, weights in zip(spans, windows, terms):
            mixed = jnp.dot(weights, v_win[m, window, :], preferred_element_type=jnp.float32)
            a_buf[u, span, :] = (mixed[:, :HEAD_WIDTH] / mixed[:, HEAD_WIDTH:]).astype(
                jnp.bfloat16
            )

    def await_inputs(chunk):
        u, part = chunk // chunks, lax.rem(chunk, chunks)
        m, g = u // per_micro, lax.rem(u, per_micro)

        @pl.when(part == 0)
        def _():
            q_load(u).wait()

        @pl.when((part == 0) & (g == 0))
        def _():
            for which in range(2):
                kv_load(m, which).wait()

        @pl.when((part == 1) & (g == 0) & (ctx > 0))
        def _():
            for which in range(2):
                halo(m, which).wait_recv()

    ones = jnp.ones((DOCMAX + rows, HEAD_WIDTH), jnp.bfloat16)
    for m in range(micro):
        v_win[m, :, pl.ds(HEAD_WIDTH, HEAD_WIDTH)] = ones

    @pl.when(ctx == 0)
    def _():
        for m in range(micro):
            for window in (k_win, v_win):
                window[m, pl.ds(0, DOCMAX), pl.ds(0, HEAD_WIDTH)] = jnp.zeros(
                    (DOCMAX, HEAD_WIDTH), jnp.bfloat16
                )

    starts_load().wait()
    mask_rows(0)

    @pl.when(pipe == 0)
    def _():
        def lead(turn):
            return jnp.minimum(FIRST + turn + jnp.minimum(turn, MORE), steps)

        @pl.loop(0, FIRST)
        def _(step):
            chunk = chunk_at(step)
            await_inputs(chunk)
            attend(chunk, 0)

        find_dest()
        pl.semaphore_wait(barrier, 2 * Z)
        dest_copy().start()
        send_halo(0)
        for step in range(FIRST):
            exchange(chunk_at(step)).start()

        @pl.loop(0, steps)
        def _(turn):
            @pl.loop(lead(turn), lead(turn + 1))
            def _(step):
                chunk = chunk_at(step)
                await_inputs(chunk)
                attend(chunk, 0)
                exchange(chunk).start()

            chunk = chunk_at(turn)
            u = chunk // chunks
            m = u // per_micro
            exchange(chunk).wait_recv()
            forward(chunk).start()

            @pl.when(lax.rem(chunk, chunks) == chunks - 1)
            def _():
                for place, source, first in ((x_lo, a_buf, 0), (1 - x_lo, b_buf, slots)):
                    picked = jnp.dot(
                        pick[m, pl.ds(first, slots), :],
                        source[u],
                        preferred_element_type=jnp.float32,
                    )
                    s_buf[u, place] = picked.astype(jnp.bfloat16).reshape(Z, CAP, CH, width)
                for to in (2, 1, 3):
                    spread_near(u, lax.rem(z + to, Z), z).start()
                keep_near(u).start()

            @pl.when(turn == 0)
            def _():
                pass_halo(0)
                dest_copy().wait()
                for whose in range(2):
                    pick_rows(0, whose, whose * slots, x_lo * slots, slots)

            @pl.when(turn == 1)
            def _():
                send_halo(1)
                mask_rows(1)

            @pl.when(turn == 3)
            def _():
                pass_halo(1)
                for whose in range(2):
                    pick_rows(1, whose, whose * slots, x_lo * slots, slots)

        pltpu.make_async_copy(a_buf, a_buf, all_send.at[0]).wait()
        pltpu.make_async_copy(b_buf, b_buf, all_send.at[1]).wait()
        sent = s_buf.at[pl.ds(0, units - units // Z)]
        pltpu.make_async_copy(sent, sent, all_send.at[2]).wait()

    @pl.when(pipe == 1)
    def _():
        find_dest()
        pl.semaphore_wait(barrier, 2 * Z)
        for m in range(micro):
            send_halo(m)
        for m in range(micro):
            pick_rows(m, 0, 0, 0, 2 * slots)
        mask_rows(1)
        for m in range(micro):
            pass_halo(m)

        @pl.loop(0, steps)
        def _(step):
            chunk = chunk_at(step)
            u = chunk // chunks
            m = u // per_micro
            await_inputs(chunk)
            forward(chunk).wait_recv()
            attend(chunk, 1)

            @pl.when(lax.rem(chunk, chunks) == chunks - 1)
            def _():
                picked = jnp.dot(pick[m], a_buf[u], preferred_element_type=jnp.float32)
                s_buf[u] = picked.astype(jnp.bfloat16).reshape(2, Z, CAP, CH, width)
                for turn in (6, 2, 5, 7, 4, 1, 3):
                    spread_far(u, lax.rem(ctx + turn, 2 * Z), ctx).start()
                keep_far(u).start()

        sent = s_buf.at[pl.ds(0, units - units // (2 * Z))]
        pltpu.make_async_copy(sent, sent, all_send.at[2]).wait()

    pltpu.make_async_copy(out_ref, out_ref, all_recv.at[0]).wait()

    @pl.when(ctx < ctx_count - 1)
    def _():
        for m in range(micro):
            for which in range(2):
                halo(m, which).wait_send()

    for m in range(micro):
        for which in range(2):
            if relay_z(m, which) != Z - 1:

                @pl.when(ctx == relay_z(m, which))
                def _():
                    from_relay(m, which).wait_send()


def local(queries, keys, values, doc_start, owners):
    _, micro, rows, width_q = queries.shape
    unit_width = HEAD_WIDTH
    units = micro * (width_q // unit_width)
    steps = units * (rows // CHUNK)
    bf16, f32, i32 = jnp.bfloat16, jnp.float32, jnp.int32
    dma = pltpu.SemaphoreType.DMA
    in_hbm = pl.BlockSpec(memory_space=pltpu.HBM)
    out = pl.pallas_call(
        kernel,
        out_shape=jax.ShapeDtypeStruct((micro, 2, Z, CAP, CH, width_q), bf16),
        in_specs=[in_hbm] * 5,
        out_specs=pl.BlockSpec(memory_space=pl.ANY),
        scratch_shapes=[
            pltpu.VMEM((units, rows, unit_width), bf16),
            pltpu.VMEM((DOCMAX, HEAD_WIDTH), bf16),
            pltpu.VMEM((units, rows, unit_width), bf16),
            pltpu.VMEM((units, rows, unit_width), bf16),
            pltpu.VMEM((units, rows, unit_width), bf16),
            pltpu.VMEM((units, 2, Z, CAP, CH, unit_width), bf16),
            pltpu.VMEM((micro, DOCMAX + rows, HEAD_WIDTH), bf16),
            pltpu.VMEM((micro, DOCMAX + rows, 2 * HEAD_WIDTH), bf16),
            pltpu.VMEM((micro, rows, SPAN), f32),
            pltpu.VMEM((micro, 2 * Z * CAP * CH, rows), bf16),
            pltpu.VMEM((2, 8, rows), i32),
            pltpu.VMEM((micro, rows), i32),
            pltpu.SMEM((micro, TRACTS_DEV), i32),
            dma((2,)),
            dma((units,)),
            dma((micro, 2)),
            dma((micro, 2)),
            dma((micro, 2)),
            dma((2,)),
            dma((2,)),
            dma((steps,)),
            dma((steps,)),
            dma((3,)),
            dma((1,)),
        ],
        compiler_params=pltpu.CompilerParams(
            collective_id=0, has_side_effects=True, vmem_limit_bytes=48 * 1024 * 1024
        ),
    )(*[pltpu.with_memory_space_constraint(a, pltpu.HBM) for a in (queries, keys, values, doc_start, owners)])
    return out.reshape(1, micro, 1, 2 * Z, CAP, CH, width_q)


def solution(mesh):
    return jax.shard_map(
        local,
        mesh=mesh,
        in_specs=(
            P("pipe", None, "ctx", "tp"),
            P("pipe", None, "ctx", "tp"),
            P("pipe", None, "ctx", "tp"),
            P(None, "ctx"),
            P(None, "ctx"),
        ),
        out_specs=P("pipe", None, "ctx", None, None, None, "tp"),
        check_vma=False,
    )
```

time: 73.2 us -> 64 us (0.87)
  Pallas kernels: 71.4 us -> 61.9 us
    pallas_call x1, Pallas kernels: 71.4 us -> 61.9 us  [local(): pl.pallas_call(kernel, out_shape=jax.ShapeDtypeStruct((micro, 2, Z, CAP,...]
where the time goes in v3:
time: 64 us; the launch traced here: 63.6 us
  Pallas kernels  61.9 us (97%)
  local copies, waits for them, and re-layouts  1.67 us (3%)
    pallas_call x1, Pallas kernels, local(): pl.pallas_call(kernel, out_shape=jax.ShapeDtypeStruct((micro, 2, Z, CAP,...  61.9 us
    unnamed x1, local copies, waits for them, and re-layouts  1.67 us

profile of v3, /device:TPU:20, one launch (start us, length us, event | category | flops | bytes accessed | tf_op | source)
XLA Modules:
  0.0 63.6 jit_solution(9646174167438947374)
XLA Ops:
  0.0 61.9 %shard_map.55 = bf16[2,2,4,3,32,1024]{5,4,3,2,1,0:T(8,128)(2,1)S(1)} custom-call(bf16[1,2,512,1024]{3,2,1,0:T(8,128)(2,1)} %q_hbm.1, bf16[1,2,512,128]{3,2,1,0:T(8,128)(2,1)} %k_hbm.1, bf16[1,2,512,128]{3,2,1,0:T(8,128)(2,1)} %v_hbm.1, s32[2,512]{1,0:T(2,128)} %starts_hbm.1, s32[2,16]{1,0:T(2,128)} %owners_hbm.1), custom_call_target="tpu_custom_call" | custom-call | tf_op jit(solution)/shard_map/pallas_call | solution.py:486
  61.9 1.7 %copy.8 = bf16[1,2,1,8,3,32,1024]{6,5,4,3,2,1,0:T(8,128)(2,1)} copy(bf16[1,2,1,8,3,32,1024]{6,5,4,3,2,1,0:T(8,128)(2,1)S(1)} %bitcast.3) | data formatting | bytes 6291456

commit v4 on v3

--- a/solution.py
+++ b/solution.py
@@ -17,7 +17,7 @@
 SPAN = BLOCK + DOCMAX
 CHUNK = 256
 EARLY = 7
-FIRST = 2
+FIRST = 1
 MORE = 4
 Z = 4
 MESH = pl.DeviceIdType.MESH
@@ -65,6 +65,7 @@
     micro = k_win.shape[0]
     per_micro = units // micro
     chunks = rows // CHUNK
+    half = chunks // 2
     steps = units * chunks
     slots = Z * CAP * CH
     scale = math.log2(math.e) / math.sqrt(HEAD_WIDTH)
@@ -74,14 +75,20 @@
     right = {"ctx": lax.rem(ctx + 1, ctx_count)}
 
     def chunk_at(step):
+        early = EARLY * half
+        later = step - early
         return jnp.where(
-            step < EARLY,
-            2 * step,
-            jnp.where(step < 2 * EARLY, 2 * (step - EARLY) + 1, step),
+            step < early,
+            step // half * chunks + lax.rem(step, half),
+            jnp.where(
+                step < 2 * early,
+                later // half * chunks + half + lax.rem(later, half),
+                step,
+            ),
         )
 
     def first_row(chunk):
-        return pl.multiple_of((1 - lax.rem(chunk, chunks)) * CHUNK, CHUNK)
+        return pl.multiple_of(lax.rem(chunk + half, chunks) * CHUNK, CHUNK)
 
     def columns(u):
         return pl.ds(pl.multiple_of(lax.rem(u, per_micro) * width, width), width)
@@ -101,7 +108,7 @@
         src, dst = ((k_hbm, k_win), (v_hbm, v_win))[which]
         return pltpu.make_async_copy(
             src.at[0, m],
-            dst.at[m, pl.ds(DOCMAX, rows), pl.ds(0, HEAD_WIDTH)],
+            dst.at[m, pl.ds(DOCMAX, rows)],
             kv_sem.at[m, which],
         )
 
@@ -109,7 +116,7 @@
         src, dst = ((k_hbm, k_win), (v_hbm, v_win))[which]
         return (
             src.at[0, m, pl.ds(rows - DOCMAX, DOCMAX)],
-            dst.at[m, pl.ds(0, DOCMAX), pl.ds(0, HEAD_WIDTH)],
+            dst.at[m, pl.ds(0, DOCMAX)],
         )
 
     def halo(m, which):
@@ -317,12 +324,11 @@
             )
             scores = scores + bias[m, span, :]
             top = jnp.max(scores, axis=1, keepdims=True)
-            terms.append(jnp.exp2((scores - top) * scale).astype(jnp.bfloat16))
-        for span, window, weights in zip(spans, windows, terms):
+            exps = jnp.exp2((scores - top) * scale)
+            terms.append((exps.astype(jnp.bfloat16), jnp.sum(exps, axis=1, keepdims=True)))
+        for span, window, (weights, denom) in zip(spans, windows, terms):
             mixed = jnp.dot(weights, v_win[m, window, :], preferred_element_type=jnp.float32)
-            a_buf[u, span, :] = (mixed[:, :HEAD_WIDTH] / mixed[:, HEAD_WIDTH:]).astype(
-                jnp.bfloat16
-            )
+            a_buf[u, span, :] = (mixed / denom).astype(jnp.bfloat16)
 
     def await_inputs(chunk):
         u, part = chunk // chunks, lax.rem(chunk, chunks)
@@ -337,20 +343,16 @@
             for which in range(2):
                 kv_load(m, which).wait()
 
-        @pl.when((part == 1) & (g == 0) & (ctx > 0))
+        @pl.when((part == half) & (g == 0) & (ctx > 0))
         def _():
             for which in range(2):
                 halo(m, which).wait_recv()
-
-    ones = jnp.ones((DOCMAX + rows, HEAD_WIDTH), jnp.bfloat16)
-    for m in range(micro):
-        v_win[m, :, pl.ds(HEAD_WIDTH, HEAD_WIDTH)] = ones
 
     @pl.when(ctx == 0)
     def _():
         for m in range(micro):
             for window in (k_win, v_win):
-                window[m, pl.ds(0, DOCMAX), pl.ds(0, HEAD_WIDTH)] = jnp.zeros(
+                window[m, pl.ds(0, DOCMAX)] = jnp.zeros(
                     (DOCMAX, HEAD_WIDTH), jnp.bfloat16
                 )
 
@@ -368,9 +370,7 @@
             await_inputs(chunk)
             attend(chunk, 0)
 
-        find_dest()
         pl.semaphore_wait(barrier, 2 * Z)
-        dest_copy().start()
         send_halo(0)
         for step in range(FIRST):
             exchange(chunk_at(step)).start()
@@ -403,23 +403,27 @@
                     spread_near(u, lax.rem(z + to, Z), z).start()
                 keep_near(u).start()
 
-            @pl.when(turn == 0)
+            @pl.when(turn == half - 1)
             def _():
                 pass_halo(0)
-                dest_copy().wait()
-                for whose in range(2):
-                    pick_rows(0, whose, whose * slots, x_lo * slots, slots)
-
-            @pl.when(turn == 1)
+                find_dest()
+                dest_copy().start()
+
+            @pl.when(turn == 2 * half - 1)
             def _():
                 send_halo(1)
                 mask_rows(1)
 
-            @pl.when(turn == 3)
+            @pl.when(turn == 4 * half - 1)
             def _():
                 pass_halo(1)
-                for whose in range(2):
-                    pick_rows(1, whose, whose * slots, x_lo * slots, slots)
+
+            @pl.when(turn == 5 * half)
+            def _():
+                dest_copy().wait()
+                for m in range(micro):
+                    for whose in range(2):
+                        pick_rows(m, whose, whose * slots, x_lo * slots, slots)
 
         pltpu.make_async_copy(a_buf, a_buf, all_send.at[0]).wait()
         pltpu.make_async_copy(b_buf, b_buf, all_send.at[1]).wait()
@@ -496,7 +500,7 @@
             pltpu.VMEM((units, rows, unit_width), bf16),
             pltpu.VMEM((units, 2, Z, CAP, CH, unit_width), bf16),
             pltpu.VMEM((micro, DOCMAX + rows, HEAD_WIDTH), bf16),
-            pltpu.VMEM((micro, DOCMAX + rows, 2 * HEAD_WIDTH), bf16),
+            pltpu.VMEM((micro, DOCMAX + rows, HEAD_WIDTH), bf16),
             pltpu.VMEM((micro, rows, SPAN), f32),
             pltpu.VMEM((micro, 2 * Z * CAP * CH, rows), bf16),
             pltpu.VMEM((2, 8, rows), i32),

time: 64 us -> 64 us (level)
  no operation moved by 1% of the time
where the time goes in v4:
time: 64 us; the launch traced here: 63.3 us
  Pallas kernels  61.6 us (96%)
  local copies, waits for them, and re-layouts  1.67 us (3%)
    pallas_call x1, Pallas kernels, local(): pl.pallas_call(kernel, out_shape=jax.ShapeDtypeStruct((micro, 2, Z, CAP,...  61.6 us
    unnamed x1, local copies, waits for them, and re-layouts  1.67 us

profile of v4, /device:TPU:20, one launch (start us, length us, event | category | flops | bytes accessed | tf_op | source)
XLA Modules:
  0.0 63.3 jit_solution(12735664857421248689)
XLA Ops:
  0.0 61.6 %shard_map.55 = bf16[2,2,4,3,32,1024]{5,4,3,2,1,0:T(8,128)(2,1)S(1)} custom-call(bf16[1,2,512,1024]{3,2,1,0:T(8,128)(2,1)} %q_hbm.1, bf16[1,2,512,128]{3,2,1,0:T(8,128)(2,1)} %k_hbm.1, bf16[1,2,512,128]{3,2,1,0:T(8,128)(2,1)} %v_hbm.1, s32[2,512]{1,0:T(2,128)} %starts_hbm.1, s32[2,16]{1,0:T(2,128)} %owners_hbm.1), custom_call_target="tpu_custom_call" | custom-call | tf_op jit(solution)/shard_map/pallas_call | solution.py:490
  61.6 1.7 %copy.8 = bf16[1,2,1,8,3,32,1024]{6,5,4,3,2,1,0:T(8,128)(2,1)} copy(bf16[1,2,1,8,3,32,1024]{6,5,4,3,2,1,0:T(8,128)(2,1)S(1)} %bitcast.3) | data formatting | bytes 6291456

commit v5 on v4

--- a/solution.py
+++ b/solution.py
@@ -16,9 +16,11 @@
 BLOCK = 128
 SPAN = BLOCK + DOCMAX
 CHUNK = 256
-EARLY = 7
+EARLY = 6
 FIRST = 1
-MORE = 4
+MORE = 6
+LATE = 4
+AHEAD = 2
 Z = 4
 MESH = pl.DeviceIdType.MESH
 MASKED = -1e30
@@ -34,6 +36,7 @@
     q_buf,
     relay,
     c_buf,
+    t_buf,
     a_buf,
     b_buf,
     s_buf,
@@ -53,6 +56,7 @@
     dest_sem,
     ex_recv,
     fw_recv,
+    cross_recv,
     all_send,
     all_recv,
 ):
@@ -74,16 +78,16 @@
     across = {"pipe": 1 - pipe, "ctx": (1 - x_lo) * Z + z}
     right = {"ctx": lax.rem(ctx + 1, ctx_count)}
 
-    def chunk_at(step):
-        early = EARLY * half
+    def chunk_at(step, skip):
+        early = (EARLY - skip) * half
         later = step - early
         return jnp.where(
             step < early,
-            step // half * chunks + lax.rem(step, half),
+            (step // half + skip) * chunks + lax.rem(step, half),
             jnp.where(
                 step < 2 * early,
-                later // half * chunks + half + lax.rem(later, half),
-                step,
+                (later // half + skip) * chunks + half + lax.rem(later, half),
+                step + skip * chunks,
             ),
         )
 
@@ -208,6 +212,28 @@
             send_sem=all_send.at[1],
             recv_sem=fw_recv.at[chunk],
             device_id=across,
+            device_id_type=MESH,
+        )
+
+    def cross(chunk):
+        u, span = chunk // chunks, pl.ds(first_row(chunk), CHUNK)
+        return pltpu.make_async_remote_copy(
+            src_ref=a_buf.at[u, span],
+            dst_ref=t_buf.at[u, span],
+            send_sem=all_send.at[1],
+            recv_sem=cross_recv.at[chunk],
+            device_id=across,
+            device_id_type=MESH,
+        )
+
+    def settle(chunk):
+        u, span = chunk // chunks, pl.ds(first_row(chunk), CHUNK)
+        return pltpu.make_async_remote_copy(
+            src_ref=t_buf.at[u, span],
+            dst_ref=c_buf.at[u, span],
+            send_sem=all_send.at[0],
+            recv_sem=fw_recv.at[chunk],
+            device_id=beside,
             device_id_type=MESH,
         )
 
@@ -361,69 +387,94 @@
 
     @pl.when(pipe == 0)
     def _():
+        turns = steps - AHEAD * chunks
+
         def lead(turn):
-            return jnp.minimum(FIRST + turn + jnp.minimum(turn, MORE), steps)
+            more = jnp.minimum(jnp.maximum(turn - 1, 0), MORE)
+            return jnp.where(
+                turn == 0, FIRST, jnp.minimum(FIRST + AHEAD * half + turn + more, steps)
+            )
+
+        def launch(chunk):
+            @pl.when(chunk < AHEAD * chunks)
+            def _():
+                cross(chunk).start()
+
+            @pl.when(chunk >= AHEAD * chunks)
+            def _():
+                exchange(chunk).start()
+
+        def consume(u):
+            m = u // per_micro
+            for place, source, first in ((x_lo, a_buf, 0), (1 - x_lo, b_buf, slots)):
+                picked = jnp.dot(
+                    pick[m, pl.ds(first, slots), :],
+                    source[u],
+                    preferred_element_type=jnp.float32,
+                )
+                s_buf[u, place] = picked.astype(jnp.bfloat16).reshape(Z, CAP, CH, width)
+            for to in (2, 1, 3):
+                spread_near(u, lax.rem(z + to, Z), z).start()
+            keep_near(u).start()
 
         @pl.loop(0, FIRST)
         def _(step):
-            chunk = chunk_at(step)
+            chunk = chunk_at(step, 0)
             await_inputs(chunk)
             attend(chunk, 0)
 
         pl.semaphore_wait(barrier, 2 * Z)
         send_halo(0)
         for step in range(FIRST):
-            exchange(chunk_at(step)).start()
-
-        @pl.loop(0, steps)
+            launch(chunk_at(jnp.int32(step), 0))
+        find_dest()
+        dest_copy().start()
+
+        @pl.loop(0, turns)
         def _(turn):
             @pl.loop(lead(turn), lead(turn + 1))
             def _(step):
-                chunk = chunk_at(step)
+                chunk = chunk_at(step, 0)
                 await_inputs(chunk)
                 attend(chunk, 0)
-                exchange(chunk).start()
-
-            chunk = chunk_at(turn)
-            u = chunk // chunks
-            m = u // per_micro
+                launch(chunk)
+
+            chunk = chunk_at(turn, AHEAD)
             exchange(chunk).wait_recv()
             forward(chunk).start()
 
             @pl.when(lax.rem(chunk, chunks) == chunks - 1)
             def _():
-                for place, source, first in ((x_lo, a_buf, 0), (1 - x_lo, b_buf, slots)):
-                    picked = jnp.dot(
-                        pick[m, pl.ds(first, slots), :],
-                        source[u],
-                        preferred_element_type=jnp.float32,
-                    )
-                    s_buf[u, place] = picked.astype(jnp.bfloat16).reshape(Z, CAP, CH, width)
-                for to in (2, 1, 3):
-                    spread_near(u, lax.rem(z + to, Z), z).start()
-                keep_near(u).start()
-
-            @pl.when(turn == half - 1)
+                consume(chunk // chunks)
+
+            @pl.when(turn == 0)
             def _():
                 pass_halo(0)
-                find_dest()
-                dest_copy().start()
-
-            @pl.when(turn == 2 * half - 1)
+
+            @pl.when(turn == 1)
             def _():
                 send_halo(1)
-                mask_rows(1)
-
-            @pl.when(turn == 4 * half - 1)
-            def _():
-                pass_halo(1)
-
-            @pl.when(turn == 5 * half)
-            def _():
                 dest_copy().wait()
                 for m in range(micro):
                     for whose in range(2):
                         pick_rows(m, whose, whose * slots, x_lo * slots, slots)
+
+            @pl.when(turn == 3)
+            def _():
+                pass_halo(1)
+                mask_rows(1)
+
+            @pl.when(turn == turns - LATE)
+            def _():
+                @pl.loop(0, AHEAD * chunks)
+                def _(left):
+                    exchange(left).start()
+
+        @pl.loop(0, AHEAD)
+        def _(u):
+            for part in range(chunks):
+                exchange(u * chunks + part).wait_recv()
+            consume(u)
 
         pltpu.make_async_copy(a_buf, a_buf, all_send.at[0]).wait()
         pltpu.make_async_copy(b_buf, b_buf, all_send.at[1]).wait()
@@ -444,10 +495,19 @@
 
         @pl.loop(0, steps)
         def _(step):
-            chunk = chunk_at(step)
+            chunk = chunk_at(step, 0)
             u = chunk // chunks
             m = u // per_micro
             await_inputs(chunk)
+
+            @pl.when(u == 0)
+            def _():
+                @pl.loop(0, AHEAD)
+                def _(other):
+                    moved = other * chunks + chunk
+                    cross(moved).wait_recv()
+                    settle(moved).start()
+
             forward(chunk).wait_recv()
             attend(chunk, 1)
 
@@ -459,6 +519,7 @@
                     spread_far(u, lax.rem(ctx + turn, 2 * Z), ctx).start()
                 keep_far(u).start()
 
+        pltpu.make_async_copy(t_buf, t_buf, all_send.at[0]).wait()
         sent = s_buf.at[pl.ds(0, units - units // (2 * Z))]
         pltpu.make_async_copy(sent, sent, all_send.at[2]).wait()
 
@@ -496,6 +557,7 @@
             pltpu.VMEM((units, rows, unit_width), bf16),
             pltpu.VMEM((DOCMAX, HEAD_WIDTH), bf16),
             pltpu.VMEM((units, rows, unit_width), bf16),
+            pltpu.VMEM((AHEAD, rows, unit_width), bf16),
             pltpu.VMEM((units, rows, unit_width), bf16),
             pltpu.VMEM((units, rows, unit_width), bf16),
             pltpu.VMEM((units, 2, Z, CAP, CH, unit_width), bf16),
@@ -515,6 +577,7 @@
             dma((2,)),
             dma((steps,)),
             dma((steps,)),
+            dma((AHEAD * (rows // CHUNK),)),
             dma((3,)),
             dma((1,)),
         ],

time: 64 us -> 62.1 us (0.970)
  Pallas kernels: 61.6 us -> 60.2 us
    pallas_call x1, Pallas kernels: 61.6 us -> 60.2 us  [local(): pl.pallas_call(kernel, out_shape=jax.ShapeDtypeStruct((micro, 2, Z, CAP,...]
where the time goes in v5:
time: 62.1 us; the launch traced here: 61.9 us
  Pallas kernels  60.2 us (97%)
  local copies, waits for them, and re-layouts  1.67 us (3%)
    pallas_call x1, Pallas kernels, local(): pl.pallas_call(kernel, out_shape=jax.ShapeDtypeStruct((micro, 2, Z, CAP,...  60.2 us
    unnamed x1, local copies, waits for them, and re-layouts  1.67 us

profile of v5, /device:TPU:20, one launch (start us, length us, event | category | flops | bytes accessed | tf_op | source)
XLA Modules:
  0.0 61.9 jit_solution(13104415628851838242)
XLA Ops:
  0.0 60.2 %shard_map.55 = bf16[2,2,4,3,32,1024]{5,4,3,2,1,0:T(8,128)(2,1)S(1)} custom-call(bf16[1,2,512,1024]{3,2,1,0:T(8,128)(2,1)} %q_hbm.1, bf16[1,2,512,128]{3,2,1,0:T(8,128)(2,1)} %k_hbm.1, bf16[1,2,512,128]{3,2,1,0:T(8,128)(2,1)} %v_hbm.1, s32[2,512]{1,0:T(2,128)} %starts_hbm.1, s32[2,16]{1,0:T(2,128)} %owners_hbm.1), custom_call_target="tpu_custom_call" | custom-call | tf_op jit(solution)/shard_map/pallas_call | solution.py:551
  60.2 1.7 %copy.8 = bf16[1,2,1,8,3,32,1024]{6,5,4,3,2,1,0:T(8,128)(2,1)} copy(bf16[1,2,1,8,3,32,1024]{6,5,4,3,2,1,0:T(8,128)(2,1)S(1)} %bitcast.3) | data formatting | bytes 6291456

commit v6 on v5

--- a/solution.py
+++ b/solution.py
@@ -425,6 +425,7 @@
 
         pl.semaphore_wait(barrier, 2 * Z)
         send_halo(0)
+        send_halo(1)
         for step in range(FIRST):
             launch(chunk_at(jnp.int32(step), 0))
         find_dest()
@@ -453,13 +454,12 @@
 
             @pl.when(turn == 1)
             def _():
-                send_halo(1)
                 dest_copy().wait()
                 for m in range(micro):
                     for whose in range(2):
                         pick_rows(m, whose, whose * slots, x_lo * slots, slots)
 
-            @pl.when(turn == 3)
+            @pl.when(turn == 2)
             def _():
                 pass_halo(1)
                 mask_rows(1)
@@ -515,8 +515,9 @@
             def _():
                 picked = jnp.dot(pick[m], a_buf[u], preferred_element_type=jnp.float32)
                 s_buf[u] = picked.astype(jnp.bfloat16).reshape(2, Z, CAP, CH, width)
-                for turn in (6, 2, 5, 7, 4, 1, 3):
-                    spread_far(u, lax.rem(ctx + turn, 2 * Z), ctx).start()
+                for other_x, turn in ((1, 2), (1, 1), (1, 3), (1, 0), (0, 2), (0, 1), (0, 3)):
+                    place = x_lo if other_x == 0 else 1 - x_lo
+                    spread_far(u, place * Z + lax.rem(z + turn, Z), ctx).start()
                 keep_far(u).start()
 
         pltpu.make_async_copy(t_buf, t_buf, all_send.at[0]).wait()

time: 62.1 us -> 61.8 us (level)
  no operation moved by 1% of the time
where the time goes in v6:
time: 61.8 us; the launch traced here: 61.5 us
  Pallas kernels  59.8 us (97%)
  local copies, waits for them, and re-layouts  1.67 us (3%)
    pallas_call x1, Pallas kernels, local(): pl.pallas_call(kernel, out_shape=jax.ShapeDtypeStruct((micro, 2, Z, CAP,...  59.8 us
    unnamed x1, local copies, waits for them, and re-layouts  1.67 us

profile of v6, /device:TPU:20, one launch (start us, length us, event | category | flops | bytes accessed | tf_op | source)
XLA Modules:
  0.0 61.5 jit_solution(13721679077181706835)
XLA Ops:
  0.0 59.8 %shard_map.55 = bf16[2,2,4,3,32,1024]{5,4,3,2,1,0:T(8,128)(2,1)S(1)} custom-call(bf16[1,2,512,1024]{3,2,1,0:T(8,128)(2,1)} %q_hbm.1, bf16[1,2,512,128]{3,2,1,0:T(8,128)(2,1)} %k_hbm.1, bf16[1,2,512,128]{3,2,1,0:T(8,128)(2,1)} %v_hbm.1, s32[2,512]{1,0:T(2,128)} %starts_hbm.1, s32[2,16]{1,0:T(2,128)} %owners_hbm.1), custom_call_target="tpu_custom_call" | custom-call | tf_op jit(solution)/shard_map/pallas_call | solution.py:552
  59.8 1.7 %copy.8 = bf16[1,2,1,8,3,32,1024]{6,5,4,3,2,1,0:T(8,128)(2,1)} copy(bf16[1,2,1,8,3,32,1024]{6,5,4,3,2,1,0:T(8,128)(2,1)S(1)} %bitcast.3) | data formatting | bytes 6291456

commit v7 on v6

--- a/solution.py
+++ b/solution.py
@@ -500,11 +500,11 @@
             m = u // per_micro
             await_inputs(chunk)
 
-            @pl.when(u == 0)
+            @pl.when((step == 0) | (step == EARLY * half - 1))
             def _():
                 @pl.loop(0, AHEAD)
                 def _(other):
-                    moved = other * chunks + chunk
+                    moved = other * chunks + jnp.where(step == 0, 0, half)
                     cross(moved).wait_recv()
                     settle(moved).start()
 

time: 61.8 us -> 61.8 us (level)
  no operation moved by 1% of the time
where the time goes in v7:
time: 61.8 us; the launch traced here: 61.4 us
  Pallas kernels  59.7 us (97%)
  local copies, waits for them, and re-layouts  1.67 us (3%)
    pallas_call x1, Pallas kernels, local(): pl.pallas_call(kernel, out_shape=jax.ShapeDtypeStruct((micro, 2, Z, CAP,...  59.7 us
    unnamed x1, local copies, waits for them, and re-layouts  1.67 us

profile of v7, /device:TPU:20, one launch (start us, length us, event | category | flops | bytes accessed | tf_op | source)
XLA Modules:
  0.0 61.4 jit_solution(1273727057032653429)
XLA Ops:
  0.0 59.7 %shard_map.55 = bf16[2,2,4,3,32,1024]{5,4,3,2,1,0:T(8,128)(2,1)S(1)} custom-call(bf16[1,2,512,1024]{3,2,1,0:T(8,128)(2,1)} %q_hbm.1, bf16[1,2,512,128]{3,2,1,0:T(8,128)(2,1)} %k_hbm.1, bf16[1,2,512,128]{3,2,1,0:T(8,128)(2,1)} %v_hbm.1, s32[2,512]{1,0:T(2,128)} %starts_hbm.1, s32[2,16]{1,0:T(2,128)} %owners_hbm.1), custom_call_target="tpu_custom_call" | custom-call | tf_op jit(solution)/shard_map/pallas_call | solution.py:552
  59.7 1.7 %copy.8 = bf16[1,2,1,8,3,32,1024]{6,5,4,3,2,1,0:T(8,128)(2,1)} copy(bf16[1,2,1,8,3,32,1024]{6,5,4,3,2,1,0:T(8,128)(2,1)S(1)} %bitcast.3) | data formatting | bytes 6291456
